TPU v7x, 128 devices: a whole 4x4x4 slice. The times are simulated.
128 devices in a mesh: role: 2 (over x_hi), dp: 64 (over x_lo, z, y, core).
Axes of the slice: x: 4 (x_hi: 2, x_lo: 2; x = x_hi * 2 + x_lo), y: 4, z: 4, core: 2. Of those that a mesh axis runs over, the one named last changes fastest.
Arguments:
- q_start: float32 [30, 16384], P(None, ('role', 'dp')), may hold values from -3 to 3
- v_start: float32 [30, 16384], P(None, ('role', 'dp')), may hold values from -6 to 6
- minv: float32 [30, 30, 16384], P(None, None, ('role', 'dp')), as said below
- geom_jac: float32 [24, 30, 16384], P(None, None, ('role', 'dp')), may hold values from -1.75 to 1.75
- pairs: int32 [2, 48, 16384], P(None, None, ('role', 'dp')), may hold values from 0 to 23, as said below
- gap_start: float32 [48, 16384], P(None, ('role', 'dp')), may hold values from -0.05 to 0.1
- actions: int32 [8, 20, 16384], P(None, None, ('role', 'dp')), may hold values from 0 to 31
- act_map: float32 [30, 20], replicated, may hold values from -1.25 to 1.25
- batch_index: int32 [128, 128, 8], P(('role', 'dp')), may hold values from 0 to 1023
- w_in: bfloat16 [108, 1024], P(None, ('role', 'dp')), may hold values from -0.625 to 0.625
- gain_one: bfloat16 [1024], P(('role', 'dp')), may hold values from 0.5 to 1.5
- w_up: bfloat16 [1024, 2048], P(('role', 'dp')), may hold values from -0.1875 to 0.1875
- w_down: bfloat16 [2048, 1024], P(('role', 'dp')), may hold values from -0.125 to 0.125
- gain_two: bfloat16 [1024], P(('role', 'dp')), may hold values from 0.5 to 1.5
- w_head: bfloat16 [1024, 21], P(('role', 'dp')), may hold values from -0.1875 to 0.1875
- log_std: float32 [20], replicated, may hold values from 0.5 to 1.2
- old_mu: float32 [131072, 20], P(('role', 'dp')), may hold values from -6 to 6
- advantage: float32 [131072], P(('role', 'dp')), may hold values from -6 to 6
- returns: float32 [131072], P(('role', 'dp')), may hold values from -6 to 6
Outputs:
- q_final: float32 [30, 16384], P(None, ('role', 'dp'))
- v_final: float32 [30, 16384], P(None, ('role', 'dp'))
- grad_w_in: float32 [108, 1024], P(None, ('role', 'dp'))
- grad_gain_one: float32 [1024], P(('role', 'dp'))
- grad_w_up: float32 [1024, 2048], P(('role', 'dp'))
- grad_w_down: float32 [2048, 1024], P(('role', 'dp'))
- grad_gain_two: float32 [1024], P(('role', 'dp'))
- grad_w_head: float32 [1024, 21], P(('role', 'dp'))
- grad_log_std: float32 [20], replicated
- mean_loss: float32 [], replicated
Inputs may be any that keep to these rules, and one draw needn't show every extreme that they name: `pairs`: the two geometries of a contact differ. `minv`: symmetric and positive definite.
All inputs are finite; a program needn't handle non-finite values.
Results may differ from a plain program's by a relative error of at most 0.02.
Values may be sent and summed in bfloat16 or wider, within the bound.
No kernel may reach another device: no remote copies, remote signals or barrier semaphores. Data moves between devices by JAX's collectives and lax.ppermute only.
A program may use at most 128 MiB of HBM per device.

v0:
```python
import math

import jax
import jax.numpy as jnp
from jax import lax
from jax.experimental import pallas as pl
from jax.experimental.pallas import tpu as pltpu
from jax.sharding import Mesh
from jax.sharding import PartitionSpec as P

EVERY = ("x", "z", "y", "c")
WIRE = ("x", "z", "y")
LANES = 128
SWAP = [(0, 1), (1, 0)]
VMEM_LIMIT = 58 * 1024 * 1024

BINS = 32
ITERS = 8
time_step = 0.02
damping = 0.5
torque = 2.0
baumgarte = 0.2
soft_reg = 0.1
clip_eps = 0.2
value_coef = 0.5
entropy_coef = 0.01
loss_scale = 1024.0

VMEM = pl.BlockSpec(memory_space=pltpu.VMEM)
SMEM = pl.BlockSpec(memory_space=pltpu.SMEM)


def dot(a, b, dims, precision=None):
    return lax.dot_general(
        a, b, (dims, ((), ())), precision=precision, preferred_element_type=jnp.float32
    )


NN = ((1,), (0,))
NT = ((1,), (1,))
TN = ((0,), (0,))


def spread(row, rows):
    return jnp.broadcast_to(row, (rows, row.shape[-1]))


def rollout_kernel(
    q_ref, v_ref, minv_ref, geom_ref, pairs_ref, gap_ref, act_ref, map_ref, picks_ref,
    q_out, v_out, rows_out,
    select, jac, mob, dela, stored,
):
    geoms, dof, envs = geom_ref.shape
    cont = gap_ref.shape[0]
    steps, acts, _ = act_ref.shape

    @pl.loop(0, geoms)
    def _(g):
        first = (pairs_ref[0] == g).astype(jnp.float32)
        select[g] = first - (pairs_ref[1] == g).astype(jnp.float32)

    def by_rows(count, many, depth, left, right, out):
        @pl.loop(0, count // many)
        def _(block):
            sums = [jnp.zeros((cont, envs), jnp.float32) for _ in range(many)]
            for k in range(depth):
                held = right(k)
                for i in range(many):
                    sums[i] = sums[i] + spread(left(k, block * many + i), cont) * held
            for i in range(many):
                out[block * many + i] = sums[i]

    by_rows(dof, 3, geoms, lambda g, d: geom_ref[g, pl.ds(d, 1), :], lambda g: select[g], jac)
    by_rows(dof, 3, dof, lambda k, d: minv_ref[d, pl.ds(k, 1), :], lambda k: jac[k], mob)
    by_rows(cont, 4, dof, lambda d, e: mob[d, pl.ds(e, 1), :], lambda d: jac[d], dela)

    denom = jnp.full((cont, envs), soft_reg, jnp.float32)
    for e in range(cont):
        denom = denom + jnp.abs(dela[e])
    inverse = 1.0 / denom
    gap_rate = baumgarte / time_step
    q_first = q_ref[...]
    gap_first = gap_ref[...] * gap_rate

    def one_step(s, carry):
        q, v, lam = carry
        level = act_ref[s].astype(jnp.float32) * (2.0 / (BINS - 1)) - 1.0
        force = torque * dot(map_ref[...], level, NN, lax.Precision.HIGHEST) - damping * v
        pushed = jnp.zeros_like(v)
        for k in range(dof):
            pushed = pushed + minv_ref[k] * spread(force[k : k + 1], dof)
        vfree = v + time_step * pushed
        drift = vfree + gap_rate * (q - q_first)
        bias = gap_first
        for d in range(dof):
            bias = bias + jac[d] * spread(drift[d : d + 1], cont)

        def sweep(_, lam):
            push = [bias, jnp.zeros_like(bias)]
            for e in range(cont):
                push[e % 2] = push[e % 2] + dela[e] * spread(lam[e : e + 1], cont)
            return jnp.maximum(lam - (push[0] + push[1]) * inverse, 0.0)

        lam = lax.fori_loop(0, ITERS, sweep, lam)
        gained = [jnp.sum(mob[d] * lam, axis=0, keepdims=True) for d in range(dof)]
        v = vfree + jnp.concatenate(gained, axis=0)
        q = q + time_step * v
        stored[s] = jnp.concatenate([q, v, lam, level], axis=0).astype(jnp.bfloat16)
        return q, v, lam

    q, v, _ = lax.fori_loop(
        0, steps, one_step, (q_first, v_ref[...], jnp.zeros((cont, envs), jnp.float32))
    )
    q_out[...] = q
    v_out[...] = v

    picks = picks_ref.shape[1]
    block = 256
    for start in range(0, picks, block):
        wanted = picks_ref[:, start : start + block]
        found = jnp.zeros((stored.shape[1], block), jnp.float32)
        for s in range(steps):
            ids = lax.broadcasted_iota(jnp.int32, (envs, block), 0) + s * envs
            hit = (ids == wanted).astype(jnp.float32).astype(jnp.bfloat16)
            found = found + dot(stored[s], hit, NN)
        rows_out[start : start + block, :] = jnp.transpose(found).astype(jnp.bfloat16)


def rollout(q_start, v_start, minv, geom_jac, pairs, gap_start, actions, act_map, picks):
    geoms, dof, envs = geom_jac.shape
    cont = gap_start.shape[0]
    steps, acts, _ = actions.shape
    row = 2 * dof + cont + acts
    return pl.pallas_call(
        rollout_kernel,
        out_shape=(
            jax.ShapeDtypeStruct((dof, envs), jnp.float32),
            jax.ShapeDtypeStruct((dof, envs), jnp.float32),
            jax.ShapeDtypeStruct((picks.shape[1], row), jnp.bfloat16),
        ),
        in_specs=[VMEM] * 9,
        out_specs=(VMEM,) * 3,
        scratch_shapes=[
            pltpu.VMEM((geoms, cont, envs), jnp.float32),
            pltpu.VMEM((dof, cont, envs), jnp.float32),
            pltpu.VMEM((dof, cont, envs), jnp.float32),
            pltpu.VMEM((cont, cont, envs), jnp.float32),
            pltpu.VMEM((steps, row, envs), jnp.bfloat16),
        ],
        compiler_params=pltpu.CompilerParams(vmem_limit_bytes=VMEM_LIMIT),
        name="rollout",
    )(q_start, v_start, minv, geom_jac, pairs, gap_start, actions, act_map, picks)


TOKEN_BLOCK = 512
HBM = pl.BlockSpec(memory_space=pl.ANY)
GELU_RATE = math.sqrt(2.0 / math.pi)
GELU_CUBE = 0.044715 * GELU_RATE


def mean_square_root(values):
    return lax.rsqrt(jnp.mean(values * values, axis=1, keepdims=True) + 1e-05)


def norm_backward(grad, values, root):
    inner = jnp.mean(grad * values, axis=1, keepdims=True)
    return root * (grad - values * (root * root * inner))


def split_by_core(core, block, rows, keep_ref, send_ref, start, lane):
    count, columns = block.shape
    groups = block.reshape(count // (2 * rows), 2, rows, columns)
    half = count // 2
    at = pl.ds(pl.multiple_of(start, half), half)
    lanes = slice(lane, lane + columns)
    for which in range(2):
        part = groups[:, which].reshape(half, columns).astype(jnp.bfloat16)

        @pl.when(core == which)
        def _():
            keep_ref[at, lanes] = part

        @pl.when(core != which)
        def _():
            send_ref[at, lanes] = part


def pack_kernel(up_ref, down_ref, in_ref, head_ref, gains_ref, out_ref):
    rows, ff = up_ref.shape
    width = down_ref.shape[1]
    obs = in_ref.shape[0]
    heads = head_ref.shape[1]
    out_ref[:, :ff] = up_ref[...]
    down = down_ref[...].astype(jnp.float32)
    out_ref[:, ff : ff + width] = down[:rows].astype(jnp.bfloat16)
    out_ref[:, ff + width : ff + 2 * width] = down[rows:].astype(jnp.bfloat16)
    first = jnp.concatenate(
        [in_ref[...].astype(jnp.float32), jnp.zeros((LANES - obs, rows), jnp.float32)], axis=0
    )
    gains = jnp.concatenate(
        [gains_ref[...].astype(jnp.float32), jnp.zeros((LANES - 2, rows), jnp.float32)], axis=0
    )
    second = pltpu.roll(jnp.transpose(gains), heads, 1)
    wide = jnp.concatenate(
        [head_ref[...].astype(jnp.float32), jnp.zeros((rows, LANES - heads), jnp.float32)], axis=1
    )
    both = jnp.concatenate([jnp.transpose(first), second + wide], axis=1)
    out_ref[:, ff + 2 * width :] = both.astype(jnp.bfloat16)


def pack(w_up, w_down, w_in, w_head, gains):
    rows, ff = w_up.shape
    width = w_down.shape[1]
    return pl.pallas_call(
        pack_kernel,
        out_shape=jax.ShapeDtypeStruct((rows, ff + 2 * width + 2 * LANES), jnp.bfloat16),
        in_specs=[VMEM] * 5,
        out_specs=VMEM,
        name="pack",
    )(w_up, w_down, w_in, w_head, gains)


def columns_in(weights_ref, parts, start, out_ref, sem):
    rows, total = weights_ref.shape
    columns = out_ref.shape[1]
    each = total // parts
    return [
        pltpu.make_async_copy(
            weights_ref.at[:, pl.ds(part * each + start, columns)],
            out_ref.at[pl.ds(part * rows, rows), :],
            sem.at[part],
        )
        for part in range(parts)
    ]


def forward_kernel(
    acts, factor, parts,
    core_ref, rows_ref, aux_ref, std_ref, weights_ref,
    keep_hbm, send_hbm, pre_hbm, dsecond_hbm, norm_hbm, down_hbm, dhead_ref, totals_ref, gains_ref,
    up_ref, both_ref, small_ref, down_ref, hidden_ref, pre_ref, dsecond_ref, norm_ref, keep_ref, send_ref,
    in_sem, out_sem,
):
    tokens = rows_ref.shape[0]
    width, ff = up_ref.shape
    load_small = columns_in(weights_ref, parts, ff + 2 * width, small_ref, in_sem.at[0])
    load_up = columns_in(weights_ref, parts, 0, up_ref, in_sem.at[1])
    load_both = columns_in(weights_ref, parts, ff, both_ref, in_sem.at[2])
    for copy in load_small + load_both + load_up:
        copy.start()

    inv_std = jnp.exp(-std_ref[...])
    lane = lax.broadcasted_iota(jnp.int32, (1, LANES), 1)
    is_act = lane < acts
    entropy = jnp.sum(jnp.where(is_act, std_ref[...], 0.0)) + 0.5 * acts * (
        1.0 + math.log(2.0 * math.pi)
    )
    dhead_ref[...] = jnp.zeros_like(dhead_ref)
    totals_ref[...] = jnp.zeros_like(totals_ref)
    low, high = 1.0 - clip_eps, 1.0 + clip_eps

    for copy in load_small:
        copy.wait()
    gains_ref[...] = jnp.transpose(small_ref[:, LANES:].astype(jnp.float32))[acts + 1 : acts + 9]
    gain_one = gains_ref[0:1, :]
    gain_two = gains_ref[1:2, :]

    many = 128
    for part, copy in enumerate(load_both):
        copy.wait()

        @pl.loop(part * (width // parts) // many, (part + 1) * (width // parts) // many)
        def _(block):
            at = pl.ds(pl.multiple_of(block * many, many), many)
            halves = both_ref[at, :].astype(jnp.float32).reshape(many // 8, 8, 2 * width)
            mixed = jnp.stack([halves[:, :, :width], halves[:, :, width:]], axis=1)
            to = pl.ds(pl.multiple_of(block * 2 * many, 2 * many), 2 * many)
            down_ref[to, :] = mixed.reshape(2 * many, width).astype(jnp.bfloat16)

    down_out = pltpu.make_async_copy(down_ref, down_hbm, out_sem.at[0])
    down_out.start()
    for copy in load_up:
        copy.wait()

    @pl.loop(0, tokens // TOKEN_BLOCK)
    def _(block):
        at = pl.ds(pl.multiple_of(block * TOKEN_BLOCK, TOKEN_BLOCK), TOKEN_BLOCK)
        rows = rows_ref[at, :]
        first = dot(rows, small_ref[:, :LANES], NT)
        norm_one = (first * mean_square_root(first) * gain_one).astype(jnp.bfloat16)
        norm_ref[at, :] = norm_one
        second = first
        chunk = 512
        for start in range(0, ff, chunk):
            lanes = slice(start, start + chunk)
            pre = dot(norm_one, up_ref[:, lanes], NN)
            pre_ref[at, lanes] = pre.astype(jnp.bfloat16)
            bent = jnp.tanh(pre * (GELU_RATE + GELU_CUBE * (pre * pre)))
            half = 0.5 * pre
            hidden = (half + half * bent).astype(jnp.bfloat16)
            hidden_ref[at, lanes] = hidden
            second = second + dot(hidden, down_ref[lanes, :], NN)
        pltpu.make_async_copy(pre_ref.at[at, :], pre_hbm.at[at, :], out_sem.at[1]).start()
        pltpu.make_async_copy(norm_ref.at[at, :], norm_hbm.at[at, :], out_sem.at[2]).start()
        root_two = mean_square_root(second)
        scaled = second * root_two
        norm_two = (scaled * gain_two).astype(jnp.bfloat16)
        head = dot(norm_two, small_ref[:, LANES:], NN)

        aux = aux_ref[at, :]
        advantage = aux[:, acts : acts + 1]
        returns = aux[:, acts + 1 : acts + 2]
        taken = pltpu.roll(rows.astype(jnp.float32), acts, 1)
        from_old = jnp.where(is_act, (taken - aux) * inv_std, 0.0)
        from_new = jnp.where(is_act, (taken - head) * inv_std, 0.0)
        apart = from_old * from_old - from_new * from_new
        ratio = jnp.exp(0.5 * jnp.sum(apart, axis=1, keepdims=True))
        free = ratio * advantage
        held = jnp.clip(ratio, low, high) * advantage
        missed = head[:, acts : acts + 1] - returns
        losses = (
            -jnp.minimum(free, held)
            + (0.5 * value_coef) * missed * missed
            - entropy_coef * entropy
        )
        on_free = jnp.where(free < held, 1.0, jnp.where(free == held, 0.5, 0.0))
        inside = jnp.where(
            (ratio > low) & (ratio < high),
            1.0,
            jnp.where((ratio == low) | (ratio == high), 0.5, 0.0),
        )
        dratio = -advantage * (on_free + (1.0 - on_free) * inside)
        dlog = (factor * dratio) * ratio
        dhead = jnp.where(
            is_act,
            dlog * (from_new * inv_std),
            jnp.where(lane == acts, (factor * value_coef) * missed, 0.0),
        )
        dstd = jnp.where(is_act, -dlog * apart - factor * entropy_coef, 0.0)
        both = jnp.where(lane == acts, losses, dstd)
        totals_ref[...] += jnp.sum(both, axis=0, keepdims=True)

        dhead = dhead.astype(jnp.bfloat16)
        dnorm = dot(dhead, small_ref[:, LANES:], NT)
        dhead_ref[0:LANES, :] += dot(dhead, norm_two, TN)
        dhead_ref[LANES : LANES + 1, :] += jnp.sum(dnorm * scaled, axis=0, keepdims=True)
        dsecond = norm_backward(dnorm * gain_two, second, root_two)
        dsecond_ref[at, :] = dsecond.astype(jnp.bfloat16)
        pltpu.make_async_copy(dsecond_ref.at[at, :], dsecond_hbm.at[at, :], out_sem.at[3]).start()

    chunk = 256

    @pl.loop(0, ff // chunk)
    def _(block):
        lanes = pl.ds(pl.multiple_of(block * chunk, chunk), chunk)
        grad = dot(hidden_ref[:, lanes], dsecond_ref[...], TN)
        start = block * (chunk // 2)
        split_by_core(core_ref[0], grad, 16, keep_ref, send_ref, start, 0)
        at = pl.ds(pl.multiple_of(start, chunk // 2), chunk // 2)
        pltpu.make_async_copy(keep_ref.at[at, :], keep_hbm.at[at, :], out_sem.at[4]).start()
        pltpu.make_async_copy(send_ref.at[at, :], send_hbm.at[at, :], out_sem.at[5]).start()

    down_out.wait()
    outs = ((pre_ref, pre_hbm), (norm_ref, norm_hbm), (dsecond_ref, dsecond_hbm))
    for place, (here, there) in enumerate(outs + ((keep_ref, keep_hbm), (send_ref, send_hbm))):
        pltpu.make_async_copy(here, there, out_sem.at[place + 1]).wait()


def forward(core, rows, aux, std, weights, ff, acts, factor):
    tokens = rows.shape[0]
    group, total = weights.shape
    width = 1024
    parts = width // group
    bf16, f32 = jnp.bfloat16, jnp.float32
    shapes = [(ff // 2, width), (ff // 2, width), (tokens, ff), (tokens, width), (tokens, width), (ff, width)]
    return pl.pallas_call(
        lambda *refs: forward_kernel(acts, factor, parts, *refs),
        out_shape=tuple(jax.ShapeDtypeStruct(shape, bf16) for shape in shapes)
        + (
            jax.ShapeDtypeStruct((LANES + 8, width), f32),
            jax.ShapeDtypeStruct((1, LANES), f32),
            jax.ShapeDtypeStruct((8, width), f32),
        ),
        in_specs=[SMEM] + [VMEM] * 3 + [HBM],
        out_specs=(HBM,) * 6 + (VMEM,) * 3,
        scratch_shapes=[
            pltpu.VMEM((width, ff), bf16),
            pltpu.VMEM((width, 2 * width), bf16),
            pltpu.VMEM((width, 2 * LANES), bf16),
            pltpu.VMEM((ff, width), bf16),
            pltpu.VMEM((tokens, ff), bf16),
            pltpu.VMEM((tokens, ff), bf16),
            pltpu.VMEM((tokens, width), bf16),
            pltpu.VMEM((tokens, width), bf16),
            pltpu.VMEM((ff // 2, width), bf16),
            pltpu.VMEM((ff // 2, width), bf16),
            pltpu.SemaphoreType.DMA((3, parts)),
            pltpu.SemaphoreType.DMA((6,)),
        ],
        compiler_params=pltpu.CompilerParams(vmem_limit_bytes=VMEM_LIMIT),
        cost_estimate=pl.CostEstimate(
            flops=6 * tokens * width * ff, bytes_accessed=30 << 20, transcendentals=tokens * ff
        ),
        name="forward",
    )(core, rows, aux, std, weights)


def backward_kernel(
    heads, parts,
    core_ref, rows_ref, weights_ref, gains_ref, pre_hbm, dsecond_hbm, norm_hbm, down_hbm, dhead_ref,
    keep_hbm, send_hbm,
    up_ref, win_ref, down_ref, pre_ref, dsecond_ref, norm_ref, dpre_ref, din_ref, dgain_ref, keep_ref, send_ref,
    in_sem, out_sem,
):
    tokens = rows_ref.shape[0]
    width, ff = up_ref.shape
    load_win = columns_in(weights_ref, parts, ff + 2 * width, win_ref, in_sem.at[0])
    load_up = columns_in(weights_ref, parts, 0, up_ref, in_sem.at[1])
    pairs = ((dsecond_hbm, dsecond_ref), (down_hbm, down_ref), (pre_hbm, pre_ref), (norm_hbm, norm_ref))
    loads = [
        pltpu.make_async_copy(there, here, in_sem.at[2, place])
        for place, (there, here) in enumerate(pairs)
    ]
    for copy in load_win + loads[:3] + load_up + loads[3:]:
        copy.start()
    gain_one = gains_ref[0:1, :]
    din_ref[...] = jnp.zeros_like(din_ref)
    dgain_ref[...] = jnp.zeros_like(dgain_ref)
    for copy in load_win + loads[:3] + load_up:
        copy.wait()

    @pl.loop(0, tokens // TOKEN_BLOCK)
    def _(block):
        at = pl.ds(pl.multiple_of(block * TOKEN_BLOCK, TOKEN_BLOCK), TOKEN_BLOCK)
        rows = rows_ref[at, :]
        first = dot(rows, win_ref[...], NT)
        root = mean_square_root(first)
        dsecond = dsecond_ref[at, :]
        dnorm = jnp.zeros((TOKEN_BLOCK, width), jnp.float32)
        chunk = 512
        for start in range(0, ff, chunk):
            lanes = slice(start, start + chunk)
            dhidden = dot(dsecond, down_ref[lanes, :], NT)
            pre = pre_ref[at, lanes].astype(jnp.float32)
            square = pre * pre
            bent = jnp.tanh(pre * (GELU_RATE + GELU_CUBE * square))
            half = 0.5 * pre
            slope = 0.5 + 0.5 * bent + (half - half * (bent * bent)) * (
                GELU_RATE + (3.0 * GELU_CUBE) * square
            )
            dpre = (dhidden * slope).astype(jnp.bfloat16)
            dpre_ref[at, lanes] = dpre
            dnorm = dnorm + dot(dpre, up_ref[:, lanes], NT)
        dgain_ref[0:1, :] += jnp.sum(dnorm * (first * root), axis=0, keepdims=True)
        dfirst = dsecond.astype(jnp.float32) + norm_backward(dnorm * gain_one, first, root)
        din_ref[...] += dot(rows, dfirst.astype(jnp.bfloat16), TN)

    loads[3].wait()
    chunk = 256
    ids = lax.broadcasted_iota(jnp.int32, (LANES, chunk), 0)

    @pl.loop(0, width // chunk)
    def _(block):
        lanes = pl.ds(pl.multiple_of(block * chunk, chunk), chunk)
        core = core_ref[0]
        half = block * (chunk // 2)
        for start in range(0, ff, 1024):
            grad = dot(norm_ref[:, lanes], dpre_ref[:, start : start + 1024], TN)
            split_by_core(core, grad, 8, keep_ref, send_ref, half, start)
        split_by_core(core, jnp.transpose(din_ref[:, lanes]), 8, keep_ref, send_ref, half, ff)
        tail = jnp.where(ids == heads, dgain_ref[0:1, lanes], dhead_ref[0:LANES, lanes])
        tail = jnp.where(ids == heads + 1, dhead_ref[LANES : LANES + 1, lanes], tail)
        split_by_core(core, jnp.transpose(tail), 8, keep_ref, send_ref, half, ff + LANES)
        at = pl.ds(pl.multiple_of(half, chunk // 2), chunk // 2)
        pltpu.make_async_copy(keep_ref.at[at, :], keep_hbm.at[at, :], out_sem.at[0]).start()
        pltpu.make_async_copy(send_ref.at[at, :], send_hbm.at[at, :], out_sem.at[1]).start()

    pltpu.make_async_copy(keep_ref, keep_hbm, out_sem.at[0]).wait()
    pltpu.make_async_copy(send_ref, send_hbm, out_sem.at[1]).wait()


def backward(heads, core, rows, weights, gains, pre, dsecond, norm_one, down, dhead):
    tokens, ff = pre.shape
    width = dsecond.shape[1]
    parts = width // weights.shape[0]
    bf16, f32 = jnp.bfloat16, jnp.float32
    out = jax.ShapeDtypeStruct((width // 2, ff + 2 * LANES), bf16)
    return pl.pallas_call(
        lambda *refs: backward_kernel(heads, parts, *refs),
        out_shape=(out, out),
        in_specs=[SMEM, VMEM, HBM, VMEM] + [HBM] * 4 + [VMEM],
        out_specs=(HBM, HBM),
        scratch_shapes=[
            pltpu.VMEM((width, ff), bf16),
            pltpu.VMEM((width, LANES), bf16),
            pltpu.VMEM((ff, width), bf16),
            pltpu.VMEM((tokens, ff), bf16),
            pltpu.VMEM((tokens, width), bf16),
            pltpu.VMEM((tokens, width), bf16),
            pltpu.VMEM((tokens, ff), bf16),
            pltpu.VMEM((LANES, width), f32),
            pltpu.VMEM((8, width), f32),
            pltpu.VMEM(out.shape, bf16),
            pltpu.VMEM(out.shape, bf16),
            pltpu.SemaphoreType.DMA((3, max(parts, 4))),
            pltpu.SemaphoreType.DMA((2,)),
        ],
        compiler_params=pltpu.CompilerParams(vmem_limit_bytes=VMEM_LIMIT),
        cost_estimate=pl.CostEstimate(
            flops=6 * tokens * width * ff, bytes_accessed=30 << 20, transcendentals=tokens * ff
        ),
        name="backward",
    )(core, rows, weights, gains, pre, dsecond, norm_one, down, dhead)


def pieces_of(values):
    first = lax.reduce_precision(values, 8, 7)
    second = lax.reduce_precision(values - first, 8, 7)
    return jnp.concatenate([first, second, values - first - second], axis=-1)


def lanes_of(*columns):
    filled = sum(c.shape[1] for c in columns)
    gap = jnp.zeros((columns[0].shape[0], LANES - filled), columns[0].dtype)
    return jnp.concatenate(columns + (gap,), axis=1)


def body(
    q_start, v_start, minv, geom_jac, pairs, gap_start, actions, act_map, batch_index,
    w_in, gain_one, w_up, w_down, gain_two, w_head, log_std, old_mu, advantage, returns,
):
    count = lax.axis_size(EVERY)
    chips = count // 2
    rows_up, ff = w_up.shape
    rows_down, width = w_down.shape
    obs = w_in.shape[0]
    heads = w_head.shape[1]
    acts = log_std.shape[0]
    per_peer = batch_index.shape[2]
    tokens = old_mu.shape[0]
    core = lax.axis_index("c").astype(jnp.int32).reshape(1)

    gains = jnp.stack([gain_one, gain_two])
    packed = pack(w_up, w_down, w_in, w_head, gains)
    beside = [packed]
    for step in (1, 3, 2):
        beside.append(lax.ppermute(packed, "x", [((i + step) % 4, i) for i in range(4)]))
    me = lax.axis_index("x")
    order = jnp.stack([beside[0], beside[1], beside[3], beside[2]])
    ordered = jnp.concatenate(
        [lax.dynamic_index_in_dim(order, (i - me) % 4, 0, keepdims=False) for i in range(4)],
        axis=1,
    )
    weights = lax.all_gather(ordered, ("z", "y", "c"), axis=0, tiled=True)

    picks = batch_index.reshape(1, count * per_peer)
    q_final, v_final, picked = rollout(
        q_start, v_start, minv, geom_jac, pairs, gap_start, actions, act_map, picks
    )
    row_width = picked.shape[1]
    arrived = lax.all_to_all(
        picked.reshape(count, per_peer, row_width), EVERY, split_axis=0, concat_axis=0, tiled=True
    )
    rows = arrived.reshape(tokens, row_width)
    aux = lanes_of(old_mu, advantage[:, None], returns[:, None])
    std = lanes_of(log_std[None])

    factor = loss_scale / (tokens * count)
    keep, send, pre, dsecond, norm_one, down, dhead, totals, gain_rows = forward(
        core, rows, aux, std, weights, ff, acts, factor
    )

    came = lax.ppermute(send, "c", SWAP)
    pair = (keep.astype(jnp.float32) + came.astype(jnp.float32)).astype(jnp.bfloat16)
    totals = totals[0, : acts + 1]
    totals = totals + lax.ppermute(totals, "c", SWAP)
    pair, dsecond = lax.optimization_barrier((pair, dsecond))
    down_came = lax.all_to_all(
        pair.reshape(chips, rows_down, width), WIRE, split_axis=0, concat_axis=0, tiled=True
    )
    grad_down = jnp.sum(down_came.astype(jnp.float32), axis=0)

    keep, send = backward(
        heads, core, rows, weights, gain_rows, pre, dsecond, norm_one, down, dhead
    )
    came = lax.ppermute(send, "c", SWAP)
    pair = (keep.astype(jnp.float32) + came.astype(jnp.float32)).reshape(chips, rows_up, -1)
    place = ff + LANES + heads + 2
    many = 3 * (acts + 1)
    line = jnp.zeros((pair.shape[2],), jnp.float32).at[place : place + many].set(pieces_of(totals))
    row_id = lax.broadcasted_iota(jnp.int32, pair.shape, 1)
    lane_id = lax.broadcasted_iota(jnp.int32, pair.shape, 2)
    special = (row_id == 0) & (lane_id >= place) & (lane_id < place + many)
    pair = jnp.where(special, line, pair).astype(jnp.bfloat16)
    up_came = lax.all_to_all(pair, WIRE, split_axis=0, concat_axis=0, tiled=True)
    summed = jnp.sum(up_came.astype(jnp.float32), axis=0)
    tail = summed[:, ff + LANES :]
    whole = summed[0, place : place + many].reshape(3, acts + 1).sum(axis=0)
    mean_loss = whole[acts] / (tokens * count)
    return (
        q_final,
        v_final,
        jnp.transpose(summed[:, ff : ff + obs]),
        tail[:, heads],
        summed[:, :ff],
        grad_down,
        tail[:, heads + 1],
        tail[:, :heads],
        whole[:acts],
        mean_loss,
    )


def solution(mesh):
    grid = Mesh(mesh.devices.reshape(4, 4, 4, 2), EVERY)
    placed = (
        P(None, EVERY),
        P(None, EVERY),
        P(None, None, EVERY),
        P(None, None, EVERY),
        P(None, None, EVERY),
        P(None, EVERY),
        P(None, None, EVERY),
        P(),
        P(EVERY, None, None),
        P(None, EVERY),
        P(EVERY),
        P(EVERY, None),
        P(EVERY, None),
        P(EVERY),
        P(EVERY, None),
        P(),
        P(EVERY, None),
        P(EVERY),
        P(EVERY),
    )
    return jax.shard_map(
        body,
        mesh=grid,
        in_specs=placed,
        out_specs=(
            P(None, EVERY),
            P(None, EVERY),
            P(None, EVERY),
            P(EVERY),
            P(EVERY, None),
            P(EVERY, None),
            P(EVERY),
            P(EVERY, None),
            P(),
            P(),
        ),
        check_vma=False,
    )
```

profile of v0, /device:TPU:0, one launch (start us, length us, event | category | flops | bytes accessed | tf_op | source)
XLA Modules:
  0.0 236.1 jit_solution(8131375349485420621)
XLA Ops:
  7.3 1.5 copy.42.in_ref
  8.7 1.2 pad_maximum_fusion.2.gains_ref
  9.9 1.6 pack.1
  11.5 1.6 collective-permute-start.2
  13.1 2.7 %collective-permute-start.1 = (bf16[8,4352]{1,0:T(8,128)(2,1)}, bf16[8,4352]{1,0:T(8,128)(2,1)S(1)}, u32[]{:S(2)}, u32[]{:S(2)}) collective-permute-start(bf16[8,4352]{1,0:T(8,128)(2,1)} %pack.1), channel_id=1, source_target_pairs={{64,0},{96,32},{0,64},{32,96},{65,1},{97,33},{1,65},{33,97},{66,2}... | collective-permute-start | bytes 208904 | tf_op jit(solution)/shard_map/ppermute | solution.py:547
  15.8 1.4 collective-permute-start
  17.2 2.2 collective-permute-done.1
  19.4 0.9 collective-permute-done
  20.3 0.9 pad_maximum_fusion
  21.3 0.7 pad_maximum_fusion.1
  22.1 0.8 copy.36.geom_ref
  22.9 0.6 copy.37.act_ref
  23.6 0.7 copy.38.map_ref
  24.4 0.7 reshape.62.picks_ref
  25.1 17.3 %rollout.1 = (f32[30,128]{1,0:T(8,128)}, f32[30,128]{1,0:T(8,128)}, bf16[1024,128]{1,0:T(8,128)(2,1)}) custom-call(f32[30,128]{1,0:T(8,128)} %q_ref.1, f32[30,128]{1,0:T(8,128)} %v_ref.1, f32[30,30,128]{2,1,0:T(8,128)} %minv_ref.1, f32[24,30,128]{2,1,0:T(8,128)} %copy.36.geom_ref, s32[2,48,128]{2,1,0:T(8,128)} %pairs_ref.1, f32[48,128]{1,0:T(8,128)} %gap_ref.1, ...), custom_call_target="tpu_custom_call" | custom-call | tf_op jit(solution)/shard_map/rollout/pallas_call | solution.py:134
  42.4 10.9 %all-to-all-start = ((bf16[128,8,128]{2,1,0:T(8,128)(2,1)}), bf16[128,8,128]{2,1,0:T(8,128)(2,1)S(1)}, u32[]{:S(2)}, u32[]{:S(2)}) async-start(bf16[128,8,128]{2,1,0:T(8,128)(2,1)} %bitcast.42), calls=%async_computation | async-start | bytes 524288 | tf_op jit(solution)/shard_map/all_to_all | solution.py:561
  54.6 1.1 maximum_maximum_fusion.refs_2_
  55.7 8.1 %all-to-all-done = bf16[128,8,128]{2,1,0:T(8,128)(2,1)S(1)} async-done(((bf16[128,8,128]{2,1,0:T(8,128)(2,1)}), bf16[128,8,128]{2,1,0:T(8,128)(2,1)S(1)}, u32[]{:S(2)}, u32[]{:S(2)}) %all-to-all-start) | async-done | bytes 262176 | tf_op jit(solution)/shard_map/all_to_all | solution.py:561
  63.8 17.0 %all-gather.2.cloned.1.call-done.refs_4_.refs_2_ = bf16[256,17408]{1,0:T(8,128)(2,1)} async-done(((bf16[8,17408]{1,0:T(8,128)(2,1)}), bf16[256,17408]{1,0:T(8,128)(2,1)}) %all-gather.2.cloned.1.call-update) | async-done | bytes 8912912 | tf_op jit(solution)/shard_map/all_gather | solution.py:554
  80.8 28.7 %forward.1 = (bf16[1024,1024]{1,0:T(8,128)(2,1)}, bf16[1024,1024]{1,0:T(8,128)(2,1)}, bf16[1024,2048]{1,0:T(8,128)(2,1)}, bf16[1024,1024]{1,0:T(8,128)(2,1)}, bf...) custom-call(s32[1]{0:T(128)} %bitcast.refs_0_, ...), custom_call_target="tpu_custom_call" | custom-call | flops 12884901888 | bytes 31457280 | tf_op jit(solution)/shard_map/forward/pallas_call | solution.py:376
  110.0 4.2 %collective-permute-done.4 = bf16[1024,1024]{1,0:T(8,128)(2,1)S(1)} collective-permute-done((bf16[1024,1024]{1,0:T(8,128)(2,1)}, bf16[1024,1024]{1,0:T(8,128)(2,1)S(1)}, u32[]{:S(2)}, u32[]{:S(2)}) %collective-permute-start.4) | collective-permute-done | bytes 2097184 | tf_op jit(solution)/shard_map/ppermute | solution.py:573
  114.2 3.9 %add_convert_fusion = bf16[1024,1024]{1,0:T(8,128)(2,1)} fusion(bf16[1024,1024]{1,0:T(8,128)(2,1)S(1)} %collective-permute-done.4, bf16[1024,1024]{1,0:T(8,128)(2,1)} %get-tuple-element.44), kind=kLoop, calls=%fused_computation.4 | loop fusion | flops 4194304 | bytes 6291456 | tf_op jit(solution)/shard_map/convert_element_type | solution.py:574
  118.1 29.1 %backward.1 = (bf16[512,2304]{1,0:T(8,128)(2,1)}, bf16[512,2304]{1,0:T(8,128)(2,1)}) custom-call(s32[1]{0:T(128)} %bitcast.refs_0_, bf16[1024,128]{1,0:T(8,128)(2,1)} %bitcast.41, bf16[256,17408]{1,0:T(8,128)(2,1)} %all-gather.2.cloned.1.call-done.refs_4_.refs_2_, f32[8,1024]{1,0:T(8,128)} %get-tuple-element.42.refs_3_, ...), custom_call_target="tpu_custom_call" | custom-call | flops 12884901888 | bytes 31457280 | tf_op jit(solution)/shard_map/backward/pallas_call | solution.py:488
  147.6 6.9 %all-to-all-start.2 = ((bf16[64,16,1024]{2,1,0:T(8,128)(2,1)}), bf16[64,16,1024]{2,1,0:T(8,128)(2,1)S(1)}, u32[]{:S(2)}, u32[]{:S(2)}) async-start(bf16[64,16,1024]{2,1,0:T(8,128)(2,1)} %bitcast.19), calls=%async_computation.2 | async-start | bytes 4194304 | tf_op jit(solution)/shard_map/all_to_all | solution.py:578
  154.6 1.1 collective-permute-done.3
  155.8 4.5 %fusion = bf16[64,8,2304]{2,1,0:T(8,128)(2,1)} fusion(bf16[512,2304]{1,0:T(8,128)(2,1)} %collective-permute-done.5, bf16[512,2304]{1,0:T(8,128)(2,1)} %get-tuple-element.51, bf16[2304]{0:T(1024)(128)(2,1)S(1)} %select_maximum_fusion, pred[2304]{0:T(1024)(128)(4,1)S(1)} %get-tuple-element.63, pred[2304]{0:T(1024)(128)(4,1)S(1)} %get-tuple-element.64, ...), kind=kLoop, calls=%fused_computation.1 | loop fusion | flops 7077888 | bytes 7087112 | tf_op jit(solution)/shard_map/convert_element_type | solution.py:594
  160.4 24.1 %all-to-all-done.2 = bf16[64,16,1024]{2,1,0:T(8,128)(2,1)S(1)} async-done(((bf16[64,16,1024]{2,1,0:T(8,128)(2,1)}), bf16[64,16,1024]{2,1,0:T(8,128)(2,1)S(1)}, u32[]{:S(2)}, u32[]{:S(2)}) %all-to-all-start.2) | async-done | bytes 2097184 | tf_op jit(solution)/shard_map/all_to_all | solution.py:578
  184.5 1.3 copy-done
  185.8 6.0 %all-to-all-start.1 = ((bf16[64,8,2304]{2,1,0:T(8,128)(2,1)}), bf16[64,8,2304]{2,1,0:T(8,128)(2,1)S(1)}, u32[]{:S(2)}, u32[]{:S(2)}) async-start(bf16[64,8,2304]{2,1,0:T(8,128)(2,1)} %fusion), calls=%async_computation.1 | async-start | bytes 4718592 | tf_op jit(solution)/shard_map/all_to_all | solution.py:595
  191.8 2.6 %convert_reduce_fusion.1 = f32[16,1024]{1,0:T(8,128)} fusion(bf16[64,16,1024]{2,1,0:T(8,128)(2,1)} %copy-done), kind=kLoop, calls=%fused_computation.3 | loop fusion | flops 2080768 | bytes 2162688 | tf_op jit(solution)/shard_map/reduce_sum | solution.py:581
  194.4 29.4 %all-to-all-done.1 = bf16[64,8,2304]{2,1,0:T(8,128)(2,1)S(1)} async-done(((bf16[64,8,2304]{2,1,0:T(8,128)(2,1)}), bf16[64,8,2304]{2,1,0:T(8,128)(2,1)S(1)}, u32[]{:S(2)}, u32[]{:S(2)}) %all-to-all-start.1) | async-done | bytes 2359328 | tf_op jit(solution)/shard_map/all_to_all | solution.py:595
  224.7 0.7 slice_reduce_fusion
  (51 shorter events, 5.5 us)
Async XLA Ops:
  7.2 14.9 %copy-start.1 = (f32[24,30,128]{2,0,1:T(8,128)S(1)}, f32[24,30,128]{2,0,1:T(8,128)}, u32[]{:S(2)}) copy-start(f32[24,30,128]{2,0,1:T(8,128)} %param.24) | copy-start | bytes 1105924
  7.2 15.7 %copy-start.4 = (s32[8,20,128]{2,0,1:T(8,128)S(1)}, s32[8,20,128]{2,0,1:T(8,128)}, u32[]{:S(2)}) copy-start(s32[8,20,128]{2,0,1:T(8,128)} %param.27) | copy-start | bytes 245764
  7.2 16.4 %copy-start.5 = (f32[30,20]{0,1:T(8,128)S(1)}, f32[30,20]{0,1:T(8,128)}, u32[]{:S(2)}) copy-start(f32[30,20]{0,1:T(8,128)} %param.28) | copy-start | bytes 7204
  7.2 17.1 %copy-start.8 = (s32[1,128,8]{1,2,0:T(8,128)S(1)}, s32[1,128,8]{1,2,0:T(8,128)}, u32[]{:S(2)}) copy-start(s32[1,128,8]{1,2,0:T(8,128)} %param.29) | copy-start | bytes 12292
  7.2 73.6 %all-gather.2.cloned.1.call-start = ((), (), s32[]{:S(2)}) async-start(), calls=%async_computation.3 | async-start | bytes 9191424 | tf_op jit(solution)/shard_map/all_gather | solution.py:554
  11.5 5.7 %collective-permute-start.2 = (bf16[8,4352]{1,0:T(8,128)(2,1)}, bf16[8,4352]{1,0:T(8,128)(2,1)S(1)}, u32[]{:S(2)}, u32[]{:S(2)}) collective-permute-start(bf16[8,4352]{1,0:T(8,128)(2,1)} %pack.1), channel_id=1, source_target_pairs={{96,0},{0,32},{32,64},{64,96},{97,1},{1,33},{33,65},{65,97},{98,2}... | collective-permute-start | bytes 208904 | tf_op jit(solution)/shard_map/ppermute | solution.py:547
  13.1 6.3 %collective-permute-start.1 = (bf16[8,4352]{1,0:T(8,128)(2,1)}, bf16[8,4352]{1,0:T(8,128)(2,1)S(1)}, u32[]{:S(2)}, u32[]{:S(2)}) collective-permute-start(bf16[8,4352]{1,0:T(8,128)(2,1)} %pack.1), channel_id=1, source_target_pairs={{64,0},{96,32},{0,64},{32,96},{65,1},{97,33},{1,65},{33,97},{66,2}... | collective-permute-start | bytes 208904 | tf_op jit(solution)/shard_map/ppermute | solution.py:547
  15.8 4.5 %collective-permute-start = (bf16[8,4352]{1,0:T(8,128)(2,1)}, bf16[8,4352]{1,0:T(8,128)(2,1)S(1)}, u32[]{:S(2)}, u32[]{:S(2)}) collective-permute-start(bf16[8,4352]{1,0:T(8,128)(2,1)} %pack.1), channel_id=1, source_target_pairs={{32,0},{64,32},{96,64},{0,96},{33,1},{65,33},{97,65},{1,97},{34,2}... | collective-permute-start | bytes 208904 | tf_op jit(solution)/shard_map/ppermute | solution.py:547
  20.3 32.9 %copy-start.6 = (f32[1024]{0:T(1024)S(1)}, f32[1024]{0:T(1024)}, u32[]{:S(2)}) copy-start(f32[1024]{0:T(1024)} %param.39) | copy-start | bytes 12292
  21.2 32.3 %copy-start.7 = (f32[1024]{0:T(1024)S(1)}, f32[1024]{0:T(1024)}, u32[]{:S(2)}) copy-start(f32[1024]{0:T(1024)} %param.38) | copy-start | bytes 12292
  21.3 32.4 %copy-start.3 = (f32[1024,20]{0,1:T(8,128)S(1)}, f32[1024,20]{0,1:T(8,128)}, u32[]{:S(2)}) copy-start(f32[1024,20]{0,1:T(8,128)} %param.37) | copy-start | bytes 245764
  22.0 31.9 %copy-start.11 = (f32[20]{0:T(128)S(1)}, f32[20]{0:T(128)}, u32[]{:S(2)}) copy-start(f32[20]{0:T(128)} %param.36) | copy-start | bytes 244
  42.4 21.4 %all-to-all-start = ((bf16[128,8,128]{2,1,0:T(8,128)(2,1)}), bf16[128,8,128]{2,1,0:T(8,128)(2,1)S(1)}, u32[]{:S(2)}, u32[]{:S(2)}) async-start(bf16[128,8,128]{2,1,0:T(8,128)(2,1)} %bitcast.42), calls=%async_computation | async-start | bytes 524288 | tf_op jit(solution)/shard_map/all_to_all | solution.py:561
  63.8 17.0 %copy-start.2 = (bf16[128,8,128]{2,1,0:T(8,128)(2,1)}, bf16[128,8,128]{2,1,0:T(8,128)(2,1)S(1)}, u32[]{:S(2)}) copy-start(bf16[128,8,128]{2,1,0:T(8,128)(2,1)S(1)} %all-to-all-done) | copy-start | bytes 786436
  109.5 4.7 %collective-permute-start.4 = (bf16[1024,1024]{1,0:T(8,128)(2,1)}, bf16[1024,1024]{1,0:T(8,128)(2,1)S(1)}, u32[]{:S(2)}, u32[]{:S(2)}) collective-permute-start(bf16[1024,1024]{1,0:T(8,128)(2,1)} %get-tuple-element.45), channel_id=1, source_target_pairs={{0,1},{1,0},{2,3},{3,2},{4,5},{5,4},{6,7},{7,6},{8,9},{9,8},{10,11... | collective-permute-start | bytes 6291464 | tf_op jit(solution)/shard_map/ppermute | solution.py:573
  147.2 7.3 %copy-start.9 = (f32[1,128]{1,0:T(1,128)S(1)}, f32[1,128]{1,0:T(1,128)}, u32[]{:S(2)}) copy-start(f32[1,128]{1,0:T(1,128)} %get-tuple-element.41) | copy-start | bytes 1540
  147.2 8.6 %collective-permute-start.5 = (bf16[512,2304]{1,0:T(8,128)(2,1)}, bf16[512,2304]{1,0:T(8,128)(2,1)}, u32[]{:S(2)}, u32[]{:S(2)}) collective-permute-start(bf16[512,2304]{1,0:T(8,128)(2,1)} %get-tuple-element.52), channel_id=1, source_target_pairs={{0,1},{1,0},{2,3},{3,2},{4,5},{5,4},{6,7},{7,6},{8,9},{9,8},{10,11... | collective-permute-start | bytes 7077896 | tf_op jit(solution)/shard_map/ppermute | solution.py:586
  147.6 36.9 %all-to-all-start.2 = ((bf16[64,16,1024]{2,1,0:T(8,128)(2,1)}), bf16[64,16,1024]{2,1,0:T(8,128)(2,1)S(1)}, u32[]{:S(2)}, u32[]{:S(2)}) async-start(bf16[64,16,1024]{2,1,0:T(8,128)(2,1)} %bitcast.19), calls=%async_computation.2 | async-start | bytes 4194304 | tf_op jit(solution)/shard_map/all_to_all | solution.py:578
  154.5 1.2 collective-permute-start.3
  184.5 1.3 copy-start
  185.8 37.9 %all-to-all-start.1 = ((bf16[64,8,2304]{2,1,0:T(8,128)(2,1)}), bf16[64,8,2304]{2,1,0:T(8,128)(2,1)S(1)}, u32[]{:S(2)}, u32[]{:S(2)}) async-start(bf16[64,8,2304]{2,1,0:T(8,128)(2,1)} %fusion), calls=%async_computation.1 | async-start | bytes 4718592 | tf_op jit(solution)/shard_map/all_to_all | solution.py:595
  226.9 1.2 copy-start.10
Sparse Core Ops, SparseCore 0:
  22.2 58.5 all-gather.1
where the time goes:
time: 237 us; the launch traced here: 236 us
  waiting for transfers between devices  86.9 us (37%)
  Pallas kernels  76.7 us (32%)
  starting transfers between devices  30.5 us (13%)
  between operations  16 us (7%)
  other arithmetic  15.5 us (7%)
  local copies, waits for them, and re-layouts  10.4 us (4%)
    all_to_all x1, waiting for transfers between devices, body(): lax.all_to_all(pair, WIRE, split_axis=0, concat_axis=0, tiled=True)  29.4 us
    pallas_call x1, Pallas kernels, backward(): pl.pallas_call(lambda *refs: backward_kernel(heads, parts, *refs), out_sh...  29.1 us
    pallas_call x1, Pallas kernels, forward(): pl.pallas_call(lambda *refs: forward_kernel(acts, factor, parts, *refs),...  28.7 us
    all_to_all x1, waiting for transfers between devices, body(): lax.all_to_all(pair.reshape(chips, rows_down, width), WIRE, split_axis=0,...  24.1 us
    pallas_call x1, Pallas kernels, rollout(): pl.pallas_call(rollout_kernel, out_shape=(jax.ShapeDtypeStruct((dof, envs...  17.3 us
    all_gather x1, waiting for transfers between devices, body(): weights = lax.all_gather(ordered, ('z', 'y', 'c'), axis=0, tiled=True)  17 us
    all_to_all x1, starting transfers between devices, body(): lax.all_to_all(picked.reshape(count, per_peer, row_width), EVERY, split_a...  10.9 us
    all_to_all x1, waiting for transfers between devices, body(): lax.all_to_all(picked.reshape(count, per_peer, row_width), EVERY, split_a...  8.12 us
  transfers between devices with their start and end apart: 10, of which 8 were waited for; matrix products, arithmetic and copies ran while one was open for 5% of the time, Pallas kernels for 7%

commit v1 on v0

--- a/solution.py
+++ b/solution.py
@@ -185,39 +185,41 @@
             send_ref[at, lanes] = part
 
 
-def pack_kernel(up_ref, down_ref, in_ref, head_ref, gains_ref, out_ref):
+def pack_kernel(up_ref, down_ref, in_ref, head_ref, one_ref, two_ref, out_ref):
     rows, ff = up_ref.shape
     width = down_ref.shape[1]
-    obs = in_ref.shape[0]
+    obs = in_ref.shape[1]
     heads = head_ref.shape[1]
+    f32 = jnp.float32
     out_ref[:, :ff] = up_ref[...]
-    down = down_ref[...].astype(jnp.float32)
+    down = down_ref[...].astype(f32)
     out_ref[:, ff : ff + width] = down[:rows].astype(jnp.bfloat16)
     out_ref[:, ff + width : ff + 2 * width] = down[rows:].astype(jnp.bfloat16)
     first = jnp.concatenate(
-        [in_ref[...].astype(jnp.float32), jnp.zeros((LANES - obs, rows), jnp.float32)], axis=0
+        [in_ref[...].astype(f32), jnp.zeros((rows, LANES - obs), f32)], axis=1
     )
     gains = jnp.concatenate(
-        [gains_ref[...].astype(jnp.float32), jnp.zeros((LANES - 2, rows), jnp.float32)], axis=0
+        [one_ref[...].astype(f32), two_ref[...].astype(f32), jnp.zeros((LANES - 2, rows), f32)],
+        axis=0,
     )
     second = pltpu.roll(jnp.transpose(gains), heads, 1)
     wide = jnp.concatenate(
-        [head_ref[...].astype(jnp.float32), jnp.zeros((rows, LANES - heads), jnp.float32)], axis=1
-    )
-    both = jnp.concatenate([jnp.transpose(first), second + wide], axis=1)
+        [head_ref[...].astype(f32), jnp.zeros((rows, LANES - heads), f32)], axis=1
+    )
+    both = jnp.concatenate([first, second + wide], axis=1)
     out_ref[:, ff + 2 * width :] = both.astype(jnp.bfloat16)
 
 
-def pack(w_up, w_down, w_in, w_head, gains):
+def pack(w_up, w_down, w_in, w_head, gain_one, gain_two):
     rows, ff = w_up.shape
     width = w_down.shape[1]
     return pl.pallas_call(
         pack_kernel,
         out_shape=jax.ShapeDtypeStruct((rows, ff + 2 * width + 2 * LANES), jnp.bfloat16),
-        in_specs=[VMEM] * 5,
+        in_specs=[VMEM] * 6,
         out_specs=VMEM,
         name="pack",
-    )(w_up, w_down, w_in, w_head, gains)
+    )(w_up, w_down, w_in, w_head, gain_one, gain_two)
 
 
 def columns_in(weights_ref, parts, start, out_ref, sem):
@@ -513,10 +515,86 @@
     )(core, rows, weights, gains, pre, dsecond, norm_one, down, dhead)
 
 
-def pieces_of(values):
-    first = lax.reduce_precision(values, 8, 7)
-    second = lax.reduce_precision(values - first, 8, 7)
-    return jnp.concatenate([first, second, values - first - second], axis=-1)
+def pair_kernel(keep_ref, came_ref, out_ref):
+    total = keep_ref[...].astype(jnp.float32) + came_ref[...].astype(jnp.float32)
+    out_ref[...] = total.astype(jnp.bfloat16)
+
+
+def pair_totals_kernel(place, count, rows, mine_ref, other_ref, keep_ref, came_ref, out_ref):
+    f32, bf16 = jnp.float32, jnp.bfloat16
+    cut = keep_ref.shape[1] - LANES
+    pair_kernel(keep_ref.at[:, :cut], came_ref.at[:, :cut], out_ref.at[:, :cut])
+    lane = lax.broadcasted_iota(jnp.int32, (8, LANES), 1)
+    totals = jnp.broadcast_to(mine_ref[...] + other_ref[...], (8, LANES))
+    totals = jnp.where(lane < count, totals, 0.0)
+    first = totals.astype(bf16).astype(f32)
+    second = (totals - first).astype(bf16).astype(f32)
+    third = totals - first - second
+    line = (
+        pltpu.roll(first, place, 1)
+        + pltpu.roll(second, place + count, 1)
+        + pltpu.roll(third, place + 2 * count, 1)
+    )
+    tail = keep_ref[:, cut:].astype(f32) + came_ref[:, cut:].astype(f32)
+    row = lax.broadcasted_iota(jnp.int32, tail.shape, 0) % rows
+    lane = lax.broadcasted_iota(jnp.int32, tail.shape, 1)
+    special = (row == 0) & (lane >= place) & (lane < place + 3 * count)
+    out_ref[:, cut:] = jnp.where(special, line[0:1], tail).astype(bf16)
+
+
+def pair_sum(keep, came, kernel=pair_kernel, small=()):
+    rows, columns = keep.shape
+    block = pl.BlockSpec((rows // 4, columns), lambda i: (i, 0))
+    whole = pl.BlockSpec((1, LANES), lambda i: (0, 0))
+    return pl.pallas_call(
+        kernel,
+        out_shape=jax.ShapeDtypeStruct(keep.shape, keep.dtype),
+        grid=(4,),
+        in_specs=[whole] * len(small) + [block, block],
+        out_specs=block,
+        compiler_params=pltpu.CompilerParams(vmem_limit_bytes=VMEM_LIMIT),
+        name="pair",
+    )(*small, keep, came)
+
+
+def finish_kernel(
+    acts, came_ref, in_ref, one_ref, up_ref, two_ref, head_ref, std_ref, loss_ref
+):
+    ff = up_ref.shape[1]
+    obs = in_ref.shape[1]
+    heads = head_ref.shape[1]
+    total = came_ref[0].astype(jnp.float32)
+    for chip in range(1, came_ref.shape[0]):
+        total = total + came_ref[chip].astype(jnp.float32)
+    up_ref[...] = total[:, :ff]
+    in_ref[...] = total[:, ff : ff + obs]
+    tail = total[:, ff + LANES :]
+    head_ref[...] = tail[:, :heads]
+    flipped = jnp.transpose(tail)
+    one_ref[...] = flipped[heads : heads + 1]
+    two_ref[...] = flipped[heads + 1 : heads + 2]
+    count = acts + 1
+    place = heads + 2
+    whole = (
+        pltpu.roll(tail, LANES - place, 1)
+        + pltpu.roll(tail, LANES - place - count, 1)
+        + pltpu.roll(tail, LANES - place - 2 * count, 1)
+    )[0:1]
+    std_ref[...] = whole[:, :acts]
+    loss_ref[...] = whole[:, acts : acts + 1]
+
+
+def finish(came, ff, obs, heads, acts):
+    rows = came.shape[1]
+    shapes = ((rows, obs), (1, rows), (rows, ff), (1, rows), (rows, heads), (1, acts), (1, 1))
+    return pl.pallas_call(
+        lambda *refs: finish_kernel(acts, *refs),
+        out_shape=tuple(jax.ShapeDtypeStruct(shape, jnp.float32) for shape in shapes),
+        in_specs=[VMEM],
+        out_specs=(VMEM,) * 7,
+        compiler_params=pltpu.CompilerParams(vmem_limit_bytes=VMEM_LIMIT),
+        name="finish",
+    )(came)
 
 
 def lanes_of(*columns):
@@ -540,8 +618,9 @@
     tokens = old_mu.shape[0]
     core = lax.axis_index("c").astype(jnp.int32).reshape(1)
 
-    gains = jnp.stack([gain_one, gain_two])
-    packed = pack(w_up, w_down, w_in, w_head, gains)
+    packed = pack(
+        w_up, w_down, jnp.transpose(w_in), w_head, gain_one.reshape(1, -1), gain_two.reshape(1, -1)
+    )
     beside = [packed]
     for step in (1, 3, 2):
         beside.append(lax.ppermute(packed, "x", [((i + step) % 4, i) for i in range(4)]))
@@ -570,44 +649,41 @@
         core, rows, aux, std, weights, ff, acts, factor
     )
 
-    came = lax.ppermute(send, "c", SWAP)
-    pair = (keep.astype(jnp.float32) + came.astype(jnp.float32)).astype(jnp.bfloat16)
-    totals = totals[0, : acts + 1]
-    totals = totals + lax.ppermute(totals, "c", SWAP)
+    pair = pair_sum(keep, lax.ppermute(send, "c", SWAP))
     pair, dsecond = lax.optimization_barrier((pair, dsecond))
     down_came = lax.all_to_all(
         pair.reshape(chips, rows_down, width), WIRE, split_axis=0, concat_axis=0, tiled=True
     )
-    grad_down = jnp.sum(down_came.astype(jnp.float32), axis=0)
-
+    other_totals = lax.ppermute(totals, "c", SWAP)
     keep, send = backward(
         heads, core, rows, weights, gain_rows, pre, dsecond, norm_one, down, dhead
     )
-    came = lax.ppermute(send, "c", SWAP)
-    pair = (keep.astype(jnp.float32) + came.astype(jnp.float32)).reshape(chips, rows_up, -1)
-    place = ff + LANES + heads + 2
-    many = 3 * (acts + 1)
-    line = jnp.zeros((pair.shape[2],), jnp.float32).at[place : place + many].set(pieces_of(totals))
-    row_id = lax.broadcasted_iota(jnp.int32, pair.shape, 1)
-    lane_id = lax.broadcasted_iota(jnp.int32, pair.shape, 2)
-    special = (row_id == 0) & (lane_id >= place) & (lane_id < place + many)
-    pair = jnp.where(special, line, pair).astype(jnp.bfloat16)
-    up_came = lax.all_to_all(pair, WIRE, split_axis=0, concat_axis=0, tiled=True)
-    summed = jnp.sum(up_came.astype(jnp.float32), axis=0)
-    tail = summed[:, ff + LANES :]
-    whole = summed[0, place : place + many].reshape(3, acts + 1).sum(axis=0)
-    mean_loss = whole[acts] / (tokens * count)
+    send, down_came = lax.optimization_barrier((send, down_came))
+    grad_down = jnp.sum(down_came.astype(jnp.float32), axis=0)
+
+    pair = pair_sum(
+        keep,
+        lax.ppermute(send, "c", SWAP),
+        lambda *refs: pair_totals_kernel(heads + 2, acts + 1, rows_up, *refs),
+        (totals, other_totals),
+    )
+    up_came = lax.all_to_all(
+        pair.reshape(chips, rows_up, -1), WIRE, split_axis=0, concat_axis=0, tiled=True
+    )
+    grad_in, grad_one, grad_up, grad_two, grad_head, grad_std, loss = finish(
+        up_came, ff, obs, heads, acts
+    )
     return (
         q_final,
         v_final,
-        jnp.transpose(summed[:, ff : ff + obs]),
-        tail[:, heads],
-        summed[:, :ff],
+        jnp.transpose(grad_in),
+        grad_one.reshape(-1),
+        grad_up,
         grad_down,
-        tail[:, heads + 1],
-        tail[:, :heads],
-        whole[:acts],
-        mean_loss,
+        grad_two.reshape(-1),
+        grad_head,
+        grad_std.reshape(-1),
+        loss.reshape(()) / (tokens * count),
     )
 
 

time: 237 us -> 220 us (0.928)
  waiting for transfers between devices: 86.9 us -> 69.3 us
  Pallas kernels: 76.7 us -> 88.6 us
  other arithmetic: 15.5 us -> 5.4 us
    all_to_all x1, waiting for transfers between devices: 24.1 us -> 0.58 us  [body(): lax.all_to_all(pair.reshape(chips, rows_down, width), WIRE, split_axis=0,...]
    pallas_call x0 -> x3, Pallas kernels: none -> 11.8 us  [the longest x2 9.1 us: pair_sum(): pl.pallas_call(kernel, out_shape=jax.ShapeDtypeStruct(keep.shape, keep.dt...]
    convert_element_type x2 -> x0, other arithmetic: 8.45 us -> none  [the longest x1 4.54 us: body(): pair = jnp.where(special, line, pair).astype(jnp.bfloat16)]
    all_to_all x1, starting transfers between devices: 5.97 us -> 9.62 us  [body(): lax.all_to_all(pair.reshape(chips, rows_up, -1), WIRE, split_axis=0, conc...]
    ppermute x3, waiting for transfers between devices: 5.26 us -> 8.39 us  [the longest x1 4.16 us: body(): pair = pair_sum(keep, lax.ppermute(send, 'c', SWAP))]
    slice x5 -> x0, local copies, waits for them, and re-layouts: 2.62 us -> none  [the longest x1 0.73 us: body(): tail[:, heads + 1]]
    unnamed x30 -> x35, local copies, waits for them, and re-layouts: 5.35 us -> 6.75 us
  transfers between devices with their start and end apart: 10 -> 10, of which waited for: 8 -> 10; matrix products, arithmetic and copies ran while one was open for 5% -> 4% of each run, Pallas kernels for 7% -> 21%
where the time goes in v1:
time: 220 us; the launch traced here: 219 us
  Pallas kernels  88.6 us (40%)
  waiting for transfers between devices  69.3 us (32%)
  starting transfers between devices  31.5 us (14%)
  between operations  16 us (7%)
  local copies, waits for them, and re-layouts  8.53 us (4%)
  other arithmetic  5.4 us (2%)
    all_to_all x1, waiting for transfers between devices, body(): lax.all_to_all(pair.reshape(chips, rows_up, -1), WIRE, split_axis=0, conc...  30 us
    pallas_call x1, Pallas kernels, backward(): pl.pallas_call(lambda *refs: backward_kernel(heads, parts, *refs), out_sh...  29.2 us
    pallas_call x1, Pallas kernels, forward(): pl.pallas_call(lambda *refs: forward_kernel(acts, factor, parts, *refs),...  28.7 us
    pallas_call x1, Pallas kernels, rollout(): pl.pallas_call(rollout_kernel, out_shape=(jax.ShapeDtypeStruct((dof, envs...  17.3 us
    all_gather x1, waiting for transfers between devices, body(): weights = lax.all_gather(ordered, ('z', 'y', 'c'), axis=0, tiled=True)  17 us
    all_to_all x1, starting transfers between devices, body(): lax.all_to_all(pair.reshape(chips, rows_up, -1), WIRE, split_axis=0, conc...  9.62 us
    all_to_all x1, starting transfers between devices, body(): lax.all_to_all(picked.reshape(count, per_peer, row_width), EVERY, split_a...  9.42 us
    pallas_call x2, Pallas kernels, pair_sum(): pl.pallas_call(kernel, out_shape=jax.ShapeDtypeStruct(keep.shape, keep.dt...  9.1 us
  transfers between devices with their start and end apart: 10, of which 10 were waited for; matrix products, arithmetic and copies ran while one was open for 4% of the time, Pallas kernels for 21%

profile of v1, /device:TPU:0, one launch (start us, length us, event | category | flops | bytes accessed | tf_op | source)
XLA Modules:
  0.0 219.3 jit_solution(7198353341302546620)
XLA Ops:
  7.3 1.6 pack.1
  8.9 2.8 %collective-permute-start = (bf16[8,4352]{1,0:T(8,128)(2,1)}, bf16[8,4352]{1,0:T(8,128)(2,1)S(1)}, u32[]{:S(2)}, u32[]{:S(2)}) collective-permute-start(bf16[8,4352]{1,0:T(8,128)(2,1)} %pack.1), channel_id=1, source_target_pairs={{32,0},{64,32},{96,64},{0,96},{33,1},{65,33},{97,65},{1,97},{34,2}... | collective-permute-start | bytes 208904 | tf_op jit(solution)/shard_map/ppermute | solution.py:626
  11.7 0.8 collective-permute-start.1
  12.5 0.9 collective-permute-start.2
  13.4 0.9 collective-permute-done
  14.4 3.5 %collective-permute-done.1 = bf16[8,4352]{1,0:T(8,128)(2,1)S(1)} collective-permute-done((bf16[8,4352]{1,0:T(8,128)(2,1)}, bf16[8,4352]{1,0:T(8,128)(2,1)S(1)}, u32[]{:S(2)}, u32[]{:S(2)}) %collective-permute-start.1) | collective-permute-done | bytes 69664 | tf_op jit(solution)/shard_map/ppermute | solution.py:626
  17.9 0.7 collective-permute-done.2
  18.6 1.0 pad_maximum_fusion
  19.6 0.7 pad_maximum_fusion.1
  20.4 0.8 copy.35.geom_ref
  21.2 0.6 copy.36.act_ref
  21.9 0.7 reshape.56.picks_ref
  22.6 0.7 copy.37.map_ref
  23.3 17.3 %rollout.1 = (f32[30,128]{1,0:T(8,128)}, f32[30,128]{1,0:T(8,128)}, bf16[1024,128]{1,0:T(8,128)(2,1)}) custom-call(f32[30,128]{1,0:T(8,128)} %q_ref.1, f32[30,128]{1,0:T(8,128)} %v_ref.1, f32[30,30,128]{2,1,0:T(8,128)} %minv_ref.1, f32[24,30,128]{2,1,0:T(8,128)} %copy.35.geom_ref, s32[2,48,128]{2,1,0:T(8,128)} %pairs_ref.1, f32[48,128]{1,0:T(8,128)} %gap_ref.1, ...), custom_call_target="tpu_custom_call" | custom-call | tf_op jit(solution)/shard_map/rollout/pallas_call | solution.py:134
  40.7 9.4 %all-to-all-start = ((bf16[128,8,128]{2,1,0:T(8,128)(2,1)}), bf16[128,8,128]{2,1,0:T(8,128)(2,1)S(1)}, u32[]{:S(2)}, u32[]{:S(2)}) async-start(bf16[128,8,128]{2,1,0:T(8,128)(2,1)} %bitcast.33), calls=%async_computation | async-start | bytes 524288 | tf_op jit(solution)/shard_map/all_to_all | solution.py:640
  51.4 1.1 maximum_maximum_fusion.refs_2_
  52.5 8.1 %all-to-all-done = bf16[128,8,128]{2,1,0:T(8,128)(2,1)S(1)} async-done(((bf16[128,8,128]{2,1,0:T(8,128)(2,1)}), bf16[128,8,128]{2,1,0:T(8,128)(2,1)S(1)}, u32[]{:S(2)}, u32[]{:S(2)}) %all-to-all-start) | async-done | bytes 262176 | tf_op jit(solution)/shard_map/all_to_all | solution.py:640
  60.7 17.0 %all-gather.2.cloned.1.call-done.refs_4_.refs_2_ = bf16[256,17408]{1,0:T(8,128)(2,1)} async-done(((bf16[8,17408]{1,0:T(8,128)(2,1)}), bf16[256,17408]{1,0:T(8,128)(2,1)}) %all-gather.2.cloned.1.call-update) | async-done | bytes 8912912 | tf_op jit(solution)/shard_map/all_gather | solution.py:633
  77.7 28.7 %forward.1 = (bf16[1024,1024]{1,0:T(8,128)(2,1)}, bf16[1024,1024]{1,0:T(8,128)(2,1)}, bf16[1024,2048]{1,0:T(8,128)(2,1)}, bf16[1024,1024]{1,0:T(8,128)(2,1)}, bf...) custom-call(s32[1]{0:T(128)} %bitcast.refs_0_, ...), custom_call_target="tpu_custom_call" | custom-call | flops 12884901888 | bytes 31457280 | tf_op jit(solution)/shard_map/forward/pallas_call | solution.py:378
  106.7 4.2 %collective-permute-done.4.came_ref = bf16[1024,1024]{1,0:T(8,128)(2,1)S(1)} collective-permute-done((bf16[1024,1024]{1,0:T(8,128)(2,1)}, bf16[1024,1024]{1,0:T(8,128)(2,1)S(1)}, u32[]{:S(2)}, u32[]{:S(2)}) %collective-permute-start.4) | collective-permute-done | bytes 2097184 | tf_op jit(solution)/shard_map/ppermute | solution.py:652
  110.9 1.4 copy-done.3
  112.2 4.3 %pair.2 = bf16[1024,1024]{1,0:T(8,128)(2,1)} custom-call(bf16[1024,1024]{1,0:T(8,128)(2,1)} %get-tuple-element.41.keep_ref, bf16[1024,1024]{1,0:T(8,128)(2,1)} %copy-done.3), custom_call_target="tpu_custom_call" | custom-call | tf_op jit(solution)/shard_map/pair/pallas_call | solution.py:549
  116.5 7.1 %all-to-all-start.1 = ((bf16[64,16,1024]{2,1,0:T(8,128)(2,1)}), bf16[64,16,1024]{2,1,0:T(8,128)(2,1)S(1)}, u32[]{:S(2)}, u32[]{:S(2)}) async-start(bf16[64,16,1024]{2,1,0:T(8,128)(2,1)} %bitcast.29), calls=%async_computation.1 | async-start | bytes 4194304 | tf_op jit(solution)/shard_map/all_to_all | solution.py:654
  123.6 29.2 %backward.1 = (bf16[512,2304]{1,0:T(8,128)(2,1)}, bf16[512,2304]{1,0:T(8,128)(2,1)}) custom-call(s32[1]{0:T(128)} %bitcast.refs_0_, bf16[1024,128]{1,0:T(8,128)(2,1)} %bitcast.32, bf16[256,17408]{1,0:T(8,128)(2,1)} %all-gather.2.cloned.1.call-done.refs_4_.refs_2_, f32[8,1024]{1,0:T(8,128)} %get-tuple-element.39.refs_3_, ...), custom_call_target="tpu_custom_call" | custom-call | flops 12884901888 | bytes 31457280 | tf_op jit(solution)/shard_map/backward/pallas_call | solution.py:490
  153.9 3.7 %collective-permute-done.3.refs_1_ = f32[1,128]{1,0:T(1,128)S(1)} collective-permute-done((f32[1,128]{1,0:T(1,128)S(1)}, f32[1,128]{1,0:T(1,128)S(1)}, u32[]{:S(2)}, u32[]{:S(2)}) %collective-permute-start.3) | collective-permute-done | bytes 544 | tf_op jit(solution)/shard_map/ppermute | solution.py:657
  158.1 1.4 copy-done.2
  159.6 4.8 %pair.3 = bf16[512,2304]{1,0:T(8,128)(2,1)} custom-call(f32[1,128]{1,0:T(1,128)} %get-tuple-element.38.refs_0_, f32[1,128]{1,0:T(1,128)} %copy-done.13, bf16[512,2304]{1,0:T(8,128)(2,1)} %get-tuple-element.48.refs_2_, bf16[512,2304]{1,0:T(8,128)(2,1)} %copy-done.2), custom_call_target="tpu_custom_call" | custom-call | tf_op jit(solution)/shard_map/pair/pallas_call | solution.py:549
  164.4 9.6 %all-to-all-start.2 = ((bf16[64,8,2304]{2,1,0:T(8,128)(2,1)}), bf16[64,8,2304]{2,1,0:T(8,128)(2,1)S(1)}, u32[]{:S(2)}, u32[]{:S(2)}) async-start(bf16[64,8,2304]{2,1,0:T(8,128)(2,1)} %bitcast.28), calls=%async_computation.2 | async-start | bytes 4718592 | tf_op jit(solution)/shard_map/all_to_all | solution.py:670
  174.0 2.6 %convert_reduce_fusion = f32[16,1024]{1,0:T(8,128)} fusion(bf16[64,16,1024]{2,1,0:T(8,128)(2,1)} %copy-done.1), kind=kLoop, calls=%fused_computation | loop fusion | flops 2080768 | bytes 2162688 | tf_op jit(solution)/shard_map/reduce_sum | solution.py:662
  176.6 30.0 %all-to-all-done.2.refs_0_ = bf16[64,8,2304]{2,1,0:T(8,128)(2,1)S(1)} async-done(((bf16[64,8,2304]{2,1,0:T(8,128)(2,1)}), bf16[64,8,2304]{2,1,0:T(8,128)(2,1)S(1)}, u32[]{:S(2)}, u32[]{:S(2)}) %all-to-all-start.2) | async-done | bytes 2359328 | tf_op jit(solution)/shard_map/all_to_all | solution.py:670
  206.7 1.4 copy-done
  208.1 2.7 %finish.1 = (f32[8,108]{1,0:T(8,128)}, f32[1,8]{1,0:T(1,128)}, f32[8,2048]{1,0:T(8,128)}, f32[1,8]{1,0:T(1,128)}, f32[8,21]{1,0:T(8,128)}, /*index=5*/f32[1,20]{1,0:T(1,128)}, f32[1,1]{1,0:T(1,128)}) custom-call(bf16[64,8,2304]{2,1,0:T(8,128)(2,1)} %copy-done), custom_call_target="tpu_custom_call" | custom-call | tf_op jit(solution)/shard_map/finish/pallas_call | solution.py:590
  (42 shorter events, 3.5 us)
Async XLA Ops:
  7.2 13.2 %copy-start.4 = (f32[24,30,128]{2,0,1:T(8,128)S(1)}, f32[24,30,128]{2,0,1:T(8,128)}, u32[]{:S(2)}) copy-start(f32[24,30,128]{2,0,1:T(8,128)} %param.22) | copy-start | bytes 1105924
  7.2 14.0 %copy-start.7 = (s32[8,20,128]{2,0,1:T(8,128)S(1)}, s32[8,20,128]{2,0,1:T(8,128)}, u32[]{:S(2)}) copy-start(s32[8,20,128]{2,0,1:T(8,128)} %param.25) | copy-start | bytes 245764
  7.2 14.6 %copy-start.11 = (s32[1,128,8]{1,2,0:T(8,128)S(1)}, s32[1,128,8]{1,2,0:T(8,128)}, u32[]{:S(2)}) copy-start(s32[1,128,8]{1,2,0:T(8,128)} %param.27) | copy-start | bytes 12292
  7.2 15.4 %copy-start.8 = (f32[30,20]{0,1:T(8,128)S(1)}, f32[30,20]{0,1:T(8,128)}, u32[]{:S(2)}) copy-start(f32[30,20]{0,1:T(8,128)} %param.26) | copy-start | bytes 7204
  7.2 70.4 %all-gather.2.cloned.1.call-start = ((), (), s32[]{:S(2)}) async-start(), calls=%async_computation.3 | async-start | bytes 9191424 | tf_op jit(solution)/shard_map/all_gather | solution.py:633
  8.9 5.5 %collective-permute-start = (bf16[8,4352]{1,0:T(8,128)(2,1)}, bf16[8,4352]{1,0:T(8,128)(2,1)S(1)}, u32[]{:S(2)}, u32[]{:S(2)}) collective-permute-start(bf16[8,4352]{1,0:T(8,128)(2,1)} %pack.1), channel_id=1, source_target_pairs={{32,0},{64,32},{96,64},{0,96},{33,1},{65,33},{97,65},{1,97},{34,2}... | collective-permute-start | bytes 208904 | tf_op jit(solution)/shard_map/ppermute | solution.py:626
  11.7 6.1 %collective-permute-start.1 = (bf16[8,4352]{1,0:T(8,128)(2,1)}, bf16[8,4352]{1,0:T(8,128)(2,1)S(1)}, u32[]{:S(2)}, u32[]{:S(2)}) collective-permute-start(bf16[8,4352]{1,0:T(8,128)(2,1)} %pack.1), channel_id=1, source_target_pairs={{64,0},{96,32},{0,64},{32,96},{65,1},{97,33},{1,65},{33,97},{66,2}... | collective-permute-start | bytes 208904 | tf_op jit(solution)/shard_map/ppermute | solution.py:626
  12.5 6.0 %collective-permute-start.2 = (bf16[8,4352]{1,0:T(8,128)(2,1)}, bf16[8,4352]{1,0:T(8,128)(2,1)S(1)}, u32[]{:S(2)}, u32[]{:S(2)}) collective-permute-start(bf16[8,4352]{1,0:T(8,128)(2,1)} %pack.1), channel_id=1, source_target_pairs={{96,0},{0,32},{32,64},{64,96},{97,1},{1,33},{33,65},{65,97},{98,2}... | collective-permute-start | bytes 208904 | tf_op jit(solution)/shard_map/ppermute | solution.py:626
  18.6 31.5 %copy-start.6 = (f32[1024,20]{0,1:T(8,128)S(1)}, f32[1024,20]{0,1:T(8,128)}, u32[]{:S(2)}) copy-start(f32[1024,20]{0,1:T(8,128)} %param.35) | copy-start | bytes 245764
  19.5 30.8 %copy-start.9 = (f32[1024]{0:T(1024)S(1)}, f32[1024]{0:T(1024)}, u32[]{:S(2)}) copy-start(f32[1024]{0:T(1024)} %param.36) | copy-start | bytes 12292
  19.6 31.0 %copy-start.10 = (f32[1024]{0:T(1024)S(1)}, f32[1024]{0:T(1024)}, u32[]{:S(2)}) copy-start(f32[1024]{0:T(1024)} %param.37) | copy-start | bytes 12292
  20.3 30.5 %copy-start.14 = (f32[20]{0:T(128)S(1)}, f32[20]{0:T(128)}, u32[]{:S(2)}) copy-start(f32[20]{0:T(128)} %param.34) | copy-start | bytes 244
  40.7 20.0 %all-to-all-start = ((bf16[128,8,128]{2,1,0:T(8,128)(2,1)}), bf16[128,8,128]{2,1,0:T(8,128)(2,1)S(1)}, u32[]{:S(2)}, u32[]{:S(2)}) async-start(bf16[128,8,128]{2,1,0:T(8,128)(2,1)} %bitcast.33), calls=%async_computation | async-start | bytes 524288 | tf_op jit(solution)/shard_map/all_to_all | solution.py:640
  60.7 17.0 %copy-start.5 = (bf16[128,8,128]{2,1,0:T(8,128)(2,1)}, bf16[128,8,128]{2,1,0:T(8,128)(2,1)S(1)}, u32[]{:S(2)}) copy-start(bf16[128,8,128]{2,1,0:T(8,128)(2,1)S(1)} %all-to-all-done) | copy-start | bytes 786436
  106.4 4.5 %collective-permute-start.4 = (bf16[1024,1024]{1,0:T(8,128)(2,1)}, bf16[1024,1024]{1,0:T(8,128)(2,1)S(1)}, u32[]{:S(2)}, u32[]{:S(2)}) collective-permute-start(bf16[1024,1024]{1,0:T(8,128)(2,1)} %get-tuple-element.42), channel_id=1, source_target_pairs={{0,1},{1,0},{2,3},{3,2},{4,5},{5,4},{6,7},{7,6},{8,9},{9,8},{10,11... | collective-permute-start | bytes 6291464 | tf_op jit(solution)/shard_map/ppermute | solution.py:652
  110.9 1.4 copy-start.3
  116.5 36.9 %all-to-all-start.1 = ((bf16[64,16,1024]{2,1,0:T(8,128)(2,1)}), bf16[64,16,1024]{2,1,0:T(8,128)(2,1)S(1)}, u32[]{:S(2)}, u32[]{:S(2)}) async-start(bf16[64,16,1024]{2,1,0:T(8,128)(2,1)} %bitcast.29), calls=%async_computation.1 | async-start | bytes 4194304 | tf_op jit(solution)/shard_map/all_to_all | solution.py:654
  123.6 29.8 %copy-start.12 = (f32[1,128]{1,0:T(1,128)S(1)}, f32[1,128]{1,0:T(1,128)}, u32[]{:S(2)}) copy-start(f32[1,128]{1,0:T(1,128)} %get-tuple-element.38.refs_0_) | copy-start | bytes 1540
  153.4 11.0 %copy-start.1 = (bf16[64,16,1024]{2,1,0:T(8,128)(2,1)}, bf16[64,16,1024]{2,1,0:T(8,128)(2,1)S(1)}, u32[]{:S(2)}) copy-start(bf16[64,16,1024]{2,1,0:T(8,128)(2,1)S(1)} %all-to-all-done.1) | copy-start | bytes 6291460
  153.4 4.7 %collective-permute-start.5 = (bf16[512,2304]{1,0:T(8,128)(2,1)}, bf16[512,2304]{1,0:T(8,128)(2,1)S(1)}, u32[]{:S(2)}, u32[]{:S(2)}) collective-permute-start(bf16[512,2304]{1,0:T(8,128)(2,1)} %get-tuple-element.51), channel_id=1, source_target_pairs={{0,1},{1,0},{2,3},{3,2},{4,5},{5,4},{6,7},{7,6},{8,9},{9,8},{10,11... | collective-permute-start | bytes 7077896 | tf_op jit(solution)/shard_map/ppermute | solution.py:666
  153.4 4.2 %collective-permute-start.3 = (f32[1,128]{1,0:T(1,128)S(1)}, f32[1,128]{1,0:T(1,128)S(1)}, u32[]{:S(2)}, u32[]{:S(2)}) collective-permute-start(f32[1,128]{1,0:T(1,128)S(1)} %copy-done.12), channel_id=1, source_target_pairs={{0,1},{1,0},{2,3},{3,2},{4,5},{5,4},{6,7},{7,6},{8,9},{9,8},{10,11... | collective-permute-start | bytes 1544 | tf_op jit(solution)/shard_map/ppermute | solution.py:657
  157.6 0.6 copy-start.13
  158.1 1.4 copy-start.2
  164.4 42.2 %all-to-all-start.2 = ((bf16[64,8,2304]{2,1,0:T(8,128)(2,1)}), bf16[64,8,2304]{2,1,0:T(8,128)(2,1)S(1)}, u32[]{:S(2)}, u32[]{:S(2)}) async-start(bf16[64,8,2304]{2,1,0:T(8,128)(2,1)} %bitcast.28), calls=%async_computation.2 | async-start | bytes 4718592 | tf_op jit(solution)/shard_map/all_to_all | solution.py:670
  206.7 1.4 copy-start
Sparse Core Ops, SparseCore 0:
  20.5 57.1 all-gather.1

commit v2 on v1

--- a/solution.py
+++ b/solution.py
@@ -12,7 +12,7 @@
 WIRE = ("x", "z", "y")
 LANES = 128
 SWAP = [(0, 1), (1, 0)]
-VMEM_LIMIT = 58 * 1024 * 1024
+VMEM_LIMIT = 46 * 1024 * 1024
 
 BINS = 32
 ITERS = 8
@@ -222,14 +222,14 @@
     )(w_up, w_down, w_in, w_head, gain_one, gain_two)
 
 
-def columns_in(weights_ref, parts, start, out_ref, sem):
+def columns_in(weights_ref, parts, first, start, out_ref, sem):
     rows, total = weights_ref.shape
     columns = out_ref.shape[1]
     each = total // parts
     return [
         pltpu.make_async_copy(
             weights_ref.at[:, pl.ds(part * each + start, columns)],
-            out_ref.at[pl.ds(part * rows, rows), :],
+            out_ref.at[pl.ds(pl.multiple_of((first + part) % parts * rows, rows), rows), :],
             sem.at[part],
         )
         for part in range(parts)
@@ -238,16 +238,16 @@
 
 def forward_kernel(
     acts, factor, parts,
-    core_ref, rows_ref, aux_ref, std_ref, weights_ref,
-    keep_hbm, send_hbm, pre_hbm, dsecond_hbm, norm_hbm, down_hbm, dhead_ref, totals_ref, gains_ref,
-    up_ref, both_ref, small_ref, down_ref, hidden_ref, pre_ref, dsecond_ref, norm_ref, keep_ref, send_ref,
+    place_ref, rows_ref, aux_ref, std_ref, weights_ref,
+    keep_ref, send_hbm, pre_hbm, dsecond_hbm, norm_hbm, down_hbm, dhead_ref, totals_ref, gains_ref,
+    up_ref, both_ref, small_ref, down_ref, hidden_ref, pre_ref, dsecond_ref, norm_ref, send_ref,
     in_sem, out_sem,
 ):
     tokens = rows_ref.shape[0]
     width, ff = up_ref.shape
-    load_small = columns_in(weights_ref, parts, ff + 2 * width, small_ref, in_sem.at[0])
-    load_up = columns_in(weights_ref, parts, 0, up_ref, in_sem.at[1])
-    load_both = columns_in(weights_ref, parts, ff, both_ref, in_sem.at[2])
+    load_small = columns_in(weights_ref, parts, place_ref[1], ff + 2 * width, small_ref, in_sem.at[0])
+    load_up = columns_in(weights_ref, parts, place_ref[1], 0, up_ref, in_sem.at[1])
+    load_both = columns_in(weights_ref, parts, place_ref[1], ff, both_ref, in_sem.at[2])
     for copy in load_small + load_both + load_up:
         copy.start()
 
@@ -271,8 +271,9 @@
     for part, copy in enumerate(load_both):
         copy.wait()
 
-        @pl.loop(part * (width // parts) // many, (part + 1) * (width // parts) // many)
-        def _(block):
+        @pl.loop(0, width // parts // many)
+        def _(step):
+            block = (place_ref[1] + part) % parts * (width // parts // many) + step
             at = pl.ds(pl.multiple_of(block * many, many), many)
             halves = both_ref[at, :].astype(jnp.float32).reshape(many // 8, 8, 2 * width)
             mixed = jnp.stack([halves[:, :, :width], halves[:, :, width:]], axis=1)
@@ -292,7 +293,7 @@
         norm_one = (first * mean_square_root(first) * gain_one).astype(jnp.bfloat16)
         norm_ref[at, :] = norm_one
         second = first
-        chunk = 512
+        chunk = 1024
         for start in range(0, ff, chunk):
             lanes = slice(start, start + chunk)
             pre = dot(norm_one, up_ref[:, lanes], NN)
@@ -350,25 +351,24 @@
         dsecond_ref[at, :] = dsecond.astype(jnp.bfloat16)
         pltpu.make_async_copy(dsecond_ref.at[at, :], dsecond_hbm.at[at, :], out_sem.at[3]).start()
 
-    chunk = 256
+    chunk = 512
 
     @pl.loop(0, ff // chunk)
     def _(block):
         lanes = pl.ds(pl.multiple_of(block * chunk, chunk), chunk)
         grad = dot(hidden_ref[:, lanes], dsecond_ref[...], TN)
         start = block * (chunk // 2)
-        split_by_core(core_ref[0], grad, 16, keep_ref, send_ref, start, 0)
+        split_by_core(place_ref[0], grad, 16, keep_ref, send_ref, start, 0)
         at = pl.ds(pl.multiple_of(start, chunk // 2), chunk // 2)
-        pltpu.make_async_copy(keep_ref.at[at, :], keep_hbm.at[at, :], out_sem.at[4]).start()
-        pltpu.make_async_copy(send_ref.at[at, :], send_hbm.at[at, :], out_sem.at[5]).start()
+        pltpu.make_async_copy(send_ref.at[at, :], send_hbm.at[at, :], out_sem.at[4]).start()
 
     down_out.wait()
     outs = ((pre_ref, pre_hbm), (norm_ref, norm_hbm), (dsecond_ref, dsecond_hbm))
-    for place, (here, there) in enumerate(outs + ((keep_ref, keep_hbm), (send_ref, send_hbm))):
+    for place, (here, there) in enumerate(outs + ((send_ref, send_hbm),)):
         pltpu.make_async_copy(here, there, out_sem.at[place + 1]).wait()
 
 
-def forward(core, rows, aux, std, weights, ff, acts, factor):
+def forward(place, rows, aux, std, weights, ff, acts, factor):
     tokens = rows.shape[0]
     group, total = weights.shape
     width = 1024
@@ -384,7 +384,7 @@
             jax.ShapeDtypeStruct((8, width), f32),
         ),
         in_specs=[SMEM] + [VMEM] * 3 + [HBM],
-        out_specs=(HBM,) * 6 + (VMEM,) * 3,
+        out_specs=(VMEM,) + (HBM,) * 5 + (VMEM,) * 3,
         scratch_shapes=[
             pltpu.VMEM((width, ff), bf16),
             pltpu.VMEM((width, 2 * width), bf16),
@@ -395,51 +395,46 @@
             pltpu.VMEM((tokens, width), bf16),
             pltpu.VMEM((tokens, width), bf16),
             pltpu.VMEM((ff // 2, width), bf16),
-            pltpu.VMEM((ff // 2, width), bf16),
             pltpu.SemaphoreType.DMA((3, parts)),
-            pltpu.SemaphoreType.DMA((6,)),
+            pltpu.SemaphoreType.DMA((5,)),
         ],
         compiler_params=pltpu.CompilerParams(vmem_limit_bytes=VMEM_LIMIT),
         cost_estimate=pl.CostEstimate(
             flops=6 * tokens * width * ff, bytes_accessed=30 << 20, transcendentals=tokens * ff
         ),
         name="forward",
-    )(core, rows, aux, std, weights)
+    )(place, rows, aux, std, weights)
 
 
 def backward_kernel(
     heads, parts,
-    core_ref, rows_ref, weights_ref, gains_ref, pre_hbm, dsecond_hbm, norm_hbm, down_hbm, dhead_ref,
-    keep_hbm, send_hbm,
-    up_ref, win_ref, down_ref, pre_ref, dsecond_ref, norm_ref, dpre_ref, din_ref, dgain_ref, keep_ref, send_ref,
+    place_ref, rows_ref, weights_ref, gains_ref, pre_hbm, dsecond_hbm, norm_hbm, down_hbm, dhead_ref,
+    keep_ref, send_hbm,
+    up_ref, win_ref, down_ref, pre_ref, dsecond_ref, norm_ref, dpre_ref, din_ref, dgain_ref, send_ref,
     in_sem, out_sem,
 ):
     tokens = rows_ref.shape[0]
     width, ff = up_ref.shape
-    load_win = columns_in(weights_ref, parts, ff + 2 * width, win_ref, in_sem.at[0])
-    load_up = columns_in(weights_ref, parts, 0, up_ref, in_sem.at[1])
+    load_win = columns_in(weights_ref, parts, place_ref[1], ff + 2 * width, win_ref, in_sem.at[0])
+    load_up = columns_in(weights_ref, parts, place_ref[1], 0, up_ref, in_sem.at[1])
     pairs = ((dsecond_hbm, dsecond_ref), (down_hbm, down_ref), (pre_hbm, pre_ref), (norm_hbm, norm_ref))
     loads = [
         pltpu.make_async_copy(there, here, in_sem.at[2, place])
         for place, (there, here) in enumerate(pairs)
     ]
-    for copy in load_win + loads[:3] + load_up + loads[3:]:
+    for copy in loads[:3] + load_win + load_up + loads[3:]:
         copy.start()
     gain_one = gains_ref[0:1, :]
     din_ref[...] = jnp.zeros_like(din_ref)
     dgain_ref[...] = jnp.zeros_like(dgain_ref)
-    for copy in load_win + loads[:3] + load_up:
+    for copy in loads[:3]:
         copy.wait()
 
     @pl.loop(0, tokens // TOKEN_BLOCK)
     def _(block):
         at = pl.ds(pl.multiple_of(block * TOKEN_BLOCK, TOKEN_BLOCK), TOKEN_BLOCK)
-        rows = rows_ref[at, :]
-        first = dot(rows, win_ref[...], NT)
-        root = mean_square_root(first)
         dsecond = dsecond_ref[at, :]
-        dnorm = jnp.zeros((TOKEN_BLOCK, width), jnp.float32)
-        chunk = 512
+        chunk = 1024
         for start in range(0, ff, chunk):
             lanes = slice(start, start + chunk)
             dhidden = dot(dsecond, down_ref[lanes, :], NT)
@@ -450,21 +445,31 @@
             slope = 0.5 + 0.5 * bent + (half - half * (bent * bent)) * (
                 GELU_RATE + (3.0 * GELU_CUBE) * square
             )
-            dpre = (dhidden * slope).astype(jnp.bfloat16)
-            dpre_ref[at, lanes] = dpre
-            dnorm = dnorm + dot(dpre, up_ref[:, lanes], NT)
+            dpre_ref[at, lanes] = (dhidden * slope).astype(jnp.bfloat16)
+
+    for copy in load_win + load_up:
+        copy.wait()
+
+    @pl.loop(0, tokens // TOKEN_BLOCK)
+    def _(block):
+        at = pl.ds(pl.multiple_of(block * TOKEN_BLOCK, TOKEN_BLOCK), TOKEN_BLOCK)
+        rows = rows_ref[at, :]
+        first = dot(rows, win_ref[...], NT)
+        root = mean_square_root(first)
+        dnorm = dot(dpre_ref[at, :], up_ref[...], NT)
         dgain_ref[0:1, :] += jnp.sum(dnorm * (first * root), axis=0, keepdims=True)
-        dfirst = dsecond.astype(jnp.float32) + norm_backward(dnorm * gain_one, first, root)
+        dfirst = dsecond_ref[at, :].astype(jnp.float32)
+        dfirst = dfirst + norm_backward(dnorm * gain_one, first, root)
         din_ref[...] += dot(rows, dfirst.astype(jnp.bfloat16), TN)
 
     loads[3].wait()
-    chunk = 256
+    chunk = 512
     ids = lax.broadcasted_iota(jnp.int32, (LANES, chunk), 0)
 
     @pl.loop(0, width // chunk)
     def _(block):
         lanes = pl.ds(pl.multiple_of(block * chunk, chunk), chunk)
-        core = core_ref[0]
+        core = place_ref[0]
         half = block * (chunk // 2)
         for start in range(0, ff, 1024):
             grad = dot(norm_ref[:, lanes], dpre_ref[:, start : start + 1024], TN)
@@ -474,14 +479,12 @@
         tail = jnp.where(ids == heads + 1, dhead_ref[LANES : LANES + 1, lanes], tail)
         split_by_core(core, jnp.transpose(tail), 8, keep_ref, send_ref, half, ff + LANES)
         at = pl.ds(pl.multiple_of(half, chunk // 2), chunk // 2)
-        pltpu.make_async_copy(keep_ref.at[at, :], keep_hbm.at[at, :], out_sem.at[0]).start()
-        pltpu.make_async_copy(send_ref.at[at, :], send_hbm.at[at, :], out_sem.at[1]).start()
-
-    pltpu.make_async_copy(keep_ref, keep_hbm, out_sem.at[0]).wait()
-    pltpu.make_async_copy(send_ref, send_hbm, out_sem.at[1]).wait()
-
-
-def backward(heads, core, rows, weights, gains, pre, dsecond, norm_one, down, dhead):
+        pltpu.make_async_copy(send_ref.at[at, :], send_hbm.at[at, :], out_sem).start()
+
+    pltpu.make_async_copy(send_ref, send_hbm, out_sem).wait()
+
+
+def backward(heads, place, rows, weights, gains, pre, dsecond, norm_one, down, dhead):
     tokens, ff = pre.shape
     width = dsecond.shape[1]
     parts = width // weights.shape[0]
@@ -491,7 +494,7 @@
         lambda *refs: backward_kernel(heads, parts, *refs),
         out_shape=(out, out),
         in_specs=[SMEM, VMEM, HBM, VMEM] + [HBM] * 4 + [VMEM],
-        out_specs=(HBM, HBM),
+        out_specs=(VMEM, HBM),
         scratch_shapes=[
             pltpu.VMEM((width, ff), bf16),
             pltpu.VMEM((width, LANES), bf16),
@@ -503,21 +506,25 @@
             pltpu.VMEM((LANES, width), f32),
             pltpu.VMEM((8, width), f32),
             pltpu.VMEM(out.shape, bf16),
-            pltpu.VMEM(out.shape, bf16),
             pltpu.SemaphoreType.DMA((3, max(parts, 4))),
-            pltpu.SemaphoreType.DMA((2,)),
+            pltpu.SemaphoreType.DMA,
         ],
         compiler_params=pltpu.CompilerParams(vmem_limit_bytes=VMEM_LIMIT),
         cost_estimate=pl.CostEstimate(
             flops=6 * tokens * width * ff, bytes_accessed=30 << 20, transcendentals=tokens * ff
         ),
         name="backward",
-    )(core, rows, weights, gains, pre, dsecond, norm_one, down, dhead)
+    )(place, rows, weights, gains, pre, dsecond, norm_one, down, dhead)
 
 
 def pair_kernel(keep_ref, came_ref, out_ref):
-    total = keep_ref[...].astype(jnp.float32) + came_ref[...].astype(jnp.float32)
-    out_ref[...] = total.astype(jnp.bfloat16)
+    many = keep_ref.shape[0] // 4
+
+    @pl.loop(0, 4)
+    def _(block):
+        at = pl.ds(pl.multiple_of(block * many, many), many)
+        total = keep_ref[at, :].astype(jnp.float32) + came_ref[at, :].astype(jnp.float32)
+        out_ref[at, :] = total.astype(jnp.bfloat16)
 
 
 def pair_totals_kernel(place, count, rows, mine_ref, other_ref, keep_ref, came_ref, out_ref):
@@ -543,16 +550,12 @@
 
 
 def pair_sum(keep, came, kernel=pair_kernel, small=()):
-    rows, columns = keep.shape
-    block = pl.BlockSpec((rows // 4, columns), lambda i: (i, 0))
-    whole = pl.BlockSpec((1, LANES), lambda i: (0, 0))
     return pl.pallas_call(
         kernel,
         out_shape=jax.ShapeDtypeStruct(keep.shape, keep.dtype),
-        grid=(4,),
-        in_specs=[whole] * len(small) + [block, block],
-        out_specs=block,
-        compiler_params=pltpu.CompilerParams(vmem_limit_bytes=VMEM_LIMIT),
+        in_specs=[VMEM] * (len(small) + 2),
+        out_specs=VMEM,
+        compiler_params=pltpu.CompilerParams(vmem_limit_bytes=VMEM_LIMIT // 3),
         name="pair",
     )(*small, keep, came)
 
@@ -592,7 +595,7 @@
         out_shape=tuple(jax.ShapeDtypeStruct(shape, jnp.float32) for shape in shapes),
         in_specs=[VMEM],
         out_specs=(VMEM,) * 7,
-        compiler_params=pltpu.CompilerParams(vmem_limit_bytes=VMEM_LIMIT),
+        compiler_params=pltpu.CompilerParams(vmem_limit_bytes=VMEM_LIMIT // 3),
         name="finish",
     )(came)
 
@@ -616,20 +619,15 @@
     acts = log_std.shape[0]
     per_peer = batch_index.shape[2]
     tokens = old_mu.shape[0]
-    core = lax.axis_index("c").astype(jnp.int32).reshape(1)
+    place = jnp.stack([lax.axis_index("c"), lax.axis_index("x")]).astype(jnp.int32)
 
     packed = pack(
         w_up, w_down, jnp.transpose(w_in), w_head, gain_one.reshape(1, -1), gain_two.reshape(1, -1)
     )
     beside = [packed]
-    for step in (1, 3, 2):
+    for step in (1, 2, 3):
         beside.append(lax.ppermute(packed, "x", [((i + step) % 4, i) for i in range(4)]))
-    me = lax.axis_index("x")
-    order = jnp.stack([beside[0], beside[1], beside[3], beside[2]])
-    ordered = jnp.concatenate(
-        [lax.dynamic_index_in_dim(order, (i - me) % 4, 0, keepdims=False) for i in range(4)],
-        axis=1,
-    )
+    ordered = jnp.concatenate(beside, axis=1)
     weights = lax.all_gather(ordered, ("z", "y", "c"), axis=0, tiled=True)
 
     picks = batch_index.reshape(1, count * per_peer)
@@ -646,7 +644,7 @@
 
     factor = loss_scale / (tokens * count)
     keep, send, pre, dsecond, norm_one, down, dhead, totals, gain_rows = forward(
-        core, rows, aux, std, weights, ff, acts, factor
+        place, rows, aux, std, weights, ff, acts, factor
     )
 
     pair = pair_sum(keep, lax.ppermute(send, "c", SWAP))
@@ -656,7 +654,7 @@
     )
     other_totals = lax.ppermute(totals, "c", SWAP)
     keep, send = backward(
-        heads, core, rows, weights, gain_rows, pre, dsecond, norm_one, down, dhead
+        heads, place, rows, weights, gain_rows, pre, dsecond, norm_one, down, dhead
     )
     send, down_came = lax.optimization_barrier((send, down_came))
     grad_down = jnp.sum(down_came.astype(jnp.float32), axis=0)

time: 220 us -> 207 us (0.941)
  Pallas kernels: 88.6 us -> 72.1 us
  local copies, waits for them, and re-layouts: 8.53 us -> 12 us
    pallas_call x2, Pallas kernels: 9.1 us -> 2.5 us  [pair_sum(): pl.pallas_call(kernel, out_shape=jax.ShapeDtypeStruct(keep.shape, keep.dt...]
    unnamed x35 -> x31, local copies, waits for them, and re-layouts: 6.75 us -> 11.4 us
    pallas_call x1, Pallas kernels: 28.7 us -> 24.8 us  [forward(): pl.pallas_call(lambda *refs: forward_kernel(acts, factor, parts, *refs),...]
    pallas_call x1, Pallas kernels: 29.2 us -> 26.2 us  [backward(): pl.pallas_call(lambda *refs: backward_kernel(heads, parts, *refs), out_sh...]
  transfers between devices with their start and end apart: 10 -> 10, of which waited for: 10 -> 10; matrix products, arithmetic and copies ran while one was open for 4% -> 4% of each run, Pallas kernels for 21% -> 20%
where the time goes in v2:
time: 207 us
  Pallas kernels  72.1 us (35%)
  waiting for transfers between devices  68.2 us (33%)
  starting transfers between devices  33.6 us (16%)
  between operations  16 us (8%)
  local copies, waits for them, and re-layouts  12 us (6%)
  other arithmetic  4.61 us (2%)
    all_to_all x1, waiting for transfers between devices, body(): lax.all_to_all(pair.reshape(chips, rows_up, -1), WIRE, split_axis=0, conc...  30 us
    pallas_call x1, Pallas kernels, backward(): pl.pallas_call(lambda *refs: backward_kernel(heads, parts, *refs), out_sh...  26.2 us
    pallas_call x1, Pallas kernels, forward(): pl.pallas_call(lambda *refs: forward_kernel(acts, factor, parts, *refs),...  24.8 us
    pallas_call x1, Pallas kernels, rollout(): pl.pallas_call(rollout_kernel, out_shape=(jax.ShapeDtypeStruct((dof, envs...  16 us
    all_gather x1, waiting for transfers between devices, body(): weights = lax.all_gather(ordered, ('z', 'y', 'c'), axis=0, tiled=True)  15.2 us
    unnamed x31, local copies, waits for them, and re-layouts  11.4 us
    all_to_all x1, starting transfers between devices, body(): lax.all_to_all(pair.reshape(chips, rows_up, -1), WIRE, split_axis=0, conc...  9.91 us
    all_to_all x1, starting transfers between devices, body(): lax.all_to_all(picked.reshape(count, per_peer, row_width), EVERY, split_a...  9.42 us
  transfers between devices with their start and end apart: 10, of which 10 were waited for; matrix products, arithmetic and copies ran while one was open for 4% of the time, Pallas kernels for 20%

profile of v2, /device:TPU:0, one launch (start us, length us, event | category | flops | bytes accessed | tf_op | source)
XLA Modules:
  0.0 206.5 jit_solution(18100899554806773425)
XLA Ops:
  7.3 1.6 pack.1
  8.9 2.8 %collective-permute-start = (bf16[8,4352]{1,0:T(8,128)(2,1)}, bf16[8,4352]{1,0:T(8,128)(2,1)S(1)}, u32[]{:S(2)}, u32[]{:S(2)}) collective-permute-start(bf16[8,4352]{1,0:T(8,128)(2,1)} %pack.1), channel_id=1, source_target_pairs={{32,0},{64,32},{96,64},{0,96},{33,1},{65,33},{97,65},{1,97},{34,2}... | collective-permute-start | bytes 208904 | tf_op jit(solution)/shard_map/ppermute | solution.py:629
  11.7 0.8 collective-permute-start.1
  12.5 0.9 collective-permute-start.2
  13.4 0.9 collective-permute-done
  14.3 3.5 %collective-permute-done.1 = bf16[8,4352]{1,0:T(8,128)(2,1)S(1)} collective-permute-done((bf16[8,4352]{1,0:T(8,128)(2,1)}, bf16[8,4352]{1,0:T(8,128)(2,1)S(1)}, u32[]{:S(2)}, u32[]{:S(2)}) %collective-permute-start.1) | collective-permute-done | bytes 69664 | tf_op jit(solution)/shard_map/ppermute | solution.py:629
  18.6 1.6 pad_maximum_fusion
  20.2 1.1 copy.35.geom_ref
  21.3 0.9 copy.36.act_ref
  22.2 0.8 copy.34
  23.1 0.8 copy.37.map_ref
  23.9 0.8 copy-done.2
  24.7 0.7 copy-done.3
  25.4 0.7 copy-done.4
  26.1 0.7 copy-done.5
  26.8 16.0 %rollout.1 = (f32[30,128]{1,0:T(8,128)}, f32[30,128]{1,0:T(8,128)}, bf16[1024,128]{1,0:T(8,128)(2,1)}) custom-call(f32[30,128]{1,0:T(8,128)S(1)} %copy-done.4, f32[30,128]{1,0:T(8,128)S(1)} %copy-done.5, f32[30,30,128]{2,1,0:T(8,128)S(1)} %copy-done.1, f32[24,30,128]{2,1,0:T(8,128)S(1)} %copy.35.geom_ref, s32[2,48,128]{2,1,0:T(8,128)S(1)} %copy-done.2, ...), custom_call_target="tpu_custom_call" | custom-call | tf_op jit(solution)/shard_map/rollout/pallas_call | solution.py:134
  42.9 9.4 %all-to-all-start = ((bf16[128,8,128]{2,1,0:T(8,128)(2,1)}), bf16[128,8,128]{2,1,0:T(8,128)(2,1)S(1)}, u32[]{:S(2)}, u32[]{:S(2)}) async-start(bf16[128,8,128]{2,1,0:T(8,128)(2,1)} %bitcast.2), calls=%async_computation | async-start | bytes 524288 | tf_op jit(solution)/shard_map/all_to_all | solution.py:638
  53.5 9.3 %all-to-all-done = bf16[128,8,128]{2,1,0:T(8,128)(2,1)S(1)} async-done(((bf16[128,8,128]{2,1,0:T(8,128)(2,1)}), bf16[128,8,128]{2,1,0:T(8,128)(2,1)S(1)}, u32[]{:S(2)}, u32[]{:S(2)}) %all-to-all-start) | async-done | bytes 262176 | tf_op jit(solution)/shard_map/all_to_all | solution.py:638
  62.9 15.2 %all-gather.2.cloned.1.call-done.refs_4_.refs_2_ = bf16[256,17408]{1,0:T(8,128)(2,1)} async-done(((bf16[8,17408]{1,0:T(8,128)(2,1)}), bf16[256,17408]{1,0:T(8,128)(2,1)}) %all-gather.2.cloned.1.call-update) | async-done | bytes 8912912 | tf_op jit(solution)/shard_map/all_gather | solution.py:631
  78.1 24.8 %forward.1 = (bf16[1024,1024]{1,0:T(8,128)(2,1)S(1)}, bf16[1024,1024]{1,0:T(8,128)(2,1)S(1)}, bf16[1024,2048]{1,0:T(8,128)(2,1)}, bf16[1024,1024]{1,0:T(8,128)(2...) custom-call(s32[2]{0:T(128)S(1)} %pad_add_fusion.refs_0_, ...), custom_call_target="tpu_custom_call" | custom-call | flops 12884901888 | bytes 31457280 | tf_op jit(solution)/shard_map/forward/pallas_call | solution.py:378
  103.3 3.9 %collective-permute-done.4.came_ref = bf16[1024,1024]{1,0:T(8,128)(2,1)S(1)} collective-permute-done((bf16[1024,1024]{1,0:T(8,128)(2,1)S(1)}, bf16[1024,1024]{1,0:T(8,128)(2,1)S(1)}, u32[]{:S(2)}, u32[]{:S(2)}) %collective-permute-start.4) | collective-permute-done | bytes 2097184 | tf_op jit(solution)/shard_map/ppermute | solution.py:650
  107.2 1.9 pair.2
  109.1 8.8 %all-to-all-start.1 = ((bf16[64,16,1024]{2,1,0:T(8,128)(2,1)}), bf16[64,16,1024]{2,1,0:T(8,128)(2,1)}, u32[]{:S(2)}, u32[]{:S(2)}) async-start(bf16[64,16,1024]{2,1,0:T(8,128)(2,1)} %bitcast.10), calls=%async_computation.1 | async-start | bytes 4194304 | tf_op jit(solution)/shard_map/all_to_all | solution.py:652
  117.9 1.6 copy-done.7
  119.5 1.6 copy-done.8
  121.1 26.2 %backward.1 = (bf16[512,2304]{1,0:T(8,128)(2,1)S(1)}, bf16[512,2304]{1,0:T(8,128)(2,1)}) custom-call(s32[2]{0:T(128)S(1)} %pad_add_fusion.refs_0_, bf16[1024,128]{1,0:T(8,128)(2,1)S(1)} %bitcast.19, bf16[256,17408]{1,0:T(8,128)(2,1)} %all-gather.2.cloned.1.call-done.refs_4_.refs_2_, f32[8,1024]{1,0:T(8,128)S(1)} %get-tuple-element.39.refs_3_, ...), custom_call_target="tpu_custom_call" | custom-call | flops 12884901888 | bytes 31457280 | tf_op jit(solution)/shard_map/backward/pallas_call | solution.py:493
  148.0 3.7 %collective-permute-done.3.refs_1_ = f32[1,128]{1,0:T(1,128)S(1)} collective-permute-done((f32[1,128]{1,0:T(1,128)S(1)}, f32[1,128]{1,0:T(1,128)S(1)}, u32[]{:S(2)}, u32[]{:S(2)}) %collective-permute-start.3) | collective-permute-done | bytes 544 | tf_op jit(solution)/shard_map/ppermute | solution.py:655
  152.9 1.4 copy-done
  154.4 9.9 %all-to-all-start.2 = ((bf16[64,8,2304]{2,1,0:T(8,128)(2,1)}), bf16[64,8,2304]{2,1,0:T(8,128)(2,1)S(1)}, u32[]{:S(2)}, u32[]{:S(2)}) async-start(bf16[64,8,2304]{2,1,0:T(8,128)(2,1)} %bitcast.17), calls=%async_computation.2 | async-start | bytes 4718592 | tf_op jit(solution)/shard_map/all_to_all | solution.py:668
  164.3 2.6 %convert_reduce_fusion = f32[16,1024]{1,0:T(8,128)} fusion(bf16[64,16,1024]{2,1,0:T(8,128)(2,1)} %all-to-all-done.1), kind=kLoop, calls=%fused_computation | loop fusion | flops 2080768 | bytes 2162688 | tf_op jit(solution)/shard_map/reduce_sum | solution.py:660
  166.9 30.0 %all-to-all-done.2.refs_0_ = bf16[64,8,2304]{2,1,0:T(8,128)(2,1)S(1)} async-done(((bf16[64,8,2304]{2,1,0:T(8,128)(2,1)}), bf16[64,8,2304]{2,1,0:T(8,128)(2,1)S(1)}, u32[]{:S(2)}, u32[]{:S(2)}) %all-to-all-start.2) | async-done | bytes 2359328 | tf_op jit(solution)/shard_map/all_to_all | solution.py:668
  196.9 1.0 finish.1
  (37 shorter events, 4.4 us)
Async XLA Ops:
  7.2 16.7 %copy-start.1 = (f32[30,30,128]{2,1,0:T(8,128)S(1)}, f32[30,30,128]{2,1,0:T(8,128)}, u32[]{:S(2)}) copy-start(f32[30,30,128]{2,1,0:T(8,128)} %minv_ref.1) | copy-start | bytes 1382404
  7.2 45.2 %copy-start.9 = (f32[1024,20]{0,1:T(8,128)S(1)}, f32[1024,20]{0,1:T(8,128)}, u32[]{:S(2)}) copy-start(f32[1024,20]{0,1:T(8,128)} %param.35) | copy-start | bytes 245764
  7.2 45.4 %copy-start.10 = (f32[1024]{0:T(1024)S(1)}, f32[1024]{0:T(1024)}, u32[]{:S(2)}) copy-start(f32[1024]{0:T(1024)} %param.36) | copy-start | bytes 12292
  7.2 70.9 %all-gather.2.cloned.1.call-start = ((), (), s32[]{:S(2)}) async-start(), calls=%async_computation.3 | async-start | bytes 9191424 | tf_op jit(solution)/shard_map/all_gather | solution.py:631
  8.9 44.0 %copy-start.11 = (f32[1024]{0:T(1024)S(1)}, f32[1024]{0:T(1024)}, u32[]{:S(2)}) copy-start(f32[1024]{0:T(1024)} %param.37) | copy-start | bytes 12292
  8.9 5.5 %collective-permute-start = (bf16[8,4352]{1,0:T(8,128)(2,1)}, bf16[8,4352]{1,0:T(8,128)(2,1)S(1)}, u32[]{:S(2)}, u32[]{:S(2)}) collective-permute-start(bf16[8,4352]{1,0:T(8,128)(2,1)} %pack.1), channel_id=1, source_target_pairs={{32,0},{64,32},{96,64},{0,96},{33,1},{65,33},{97,65},{1,97},{34,2}... | collective-permute-start | bytes 208904 | tf_op jit(solution)/shard_map/ppermute | solution.py:629
  11.7 6.1 %collective-permute-start.1 = (bf16[8,4352]{1,0:T(8,128)(2,1)}, bf16[8,4352]{1,0:T(8,128)(2,1)S(1)}, u32[]{:S(2)}, u32[]{:S(2)}) collective-permute-start(bf16[8,4352]{1,0:T(8,128)(2,1)} %pack.1), channel_id=1, source_target_pairs={{64,0},{96,32},{0,64},{32,96},{65,1},{97,33},{1,65},{33,97},{66,2}... | collective-permute-start | bytes 208904 | tf_op jit(solution)/shard_map/ppermute | solution.py:629
  12.5 6.0 %collective-permute-start.2 = (bf16[8,4352]{1,0:T(8,128)(2,1)}, bf16[8,4352]{1,0:T(8,128)(2,1)S(1)}, u32[]{:S(2)}, u32[]{:S(2)}) collective-permute-start(bf16[8,4352]{1,0:T(8,128)(2,1)} %pack.1), channel_id=1, source_target_pairs={{96,0},{0,32},{32,64},{64,96},{97,1},{1,33},{33,65},{65,97},{98,2}... | collective-permute-start | bytes 208904 | tf_op jit(solution)/shard_map/ppermute | solution.py:629
  20.2 32.9 %copy-start.12 = (f32[20]{0:T(128)S(1)}, f32[20]{0:T(128)}, u32[]{:S(2)}) copy-start(f32[20]{0:T(128)} %param.34) | copy-start | bytes 244
  23.9 0.8 copy-start.2
  24.7 0.7 copy-start.3
  25.4 0.7 copy-start.4
  26.1 0.7 copy-start.5
  42.9 20.0 %all-to-all-start = ((bf16[128,8,128]{2,1,0:T(8,128)(2,1)}), bf16[128,8,128]{2,1,0:T(8,128)(2,1)S(1)}, u32[]{:S(2)}, u32[]{:S(2)}) async-start(bf16[128,8,128]{2,1,0:T(8,128)(2,1)} %bitcast.2), calls=%async_computation | async-start | bytes 524288 | tf_op jit(solution)/shard_map/all_to_all | solution.py:638
  103.0 6.1 %copy-start.6 = (bf16[1024,1024]{1,0:T(8,128)(2,1)}, bf16[1024,1024]{1,0:T(8,128)(2,1)S(1)}, u32[]{:S(2)}) copy-start(bf16[1024,1024]{1,0:T(8,128)(2,1)S(1)} %get-tuple-element.44.refs_5_) | copy-start | bytes 6291460
  103.0 4.2 %collective-permute-start.4 = (bf16[1024,1024]{1,0:T(8,128)(2,1)S(1)}, bf16[1024,1024]{1,0:T(8,128)(2,1)S(1)}, u32[]{:S(2)}, u32[]{:S(2)}) collective-permute-start(bf16[1024,1024]{1,0:T(8,128)(2,1)S(1)} %get-tuple-element.42), channel_id=1, source_target_pairs={{0,1},{1,0},{2,3},{3,2},{4,5},{5,4},{6,7},{7,6},{8,9},{9,8},{10,11... | collective-permute-start | bytes 6291464 | tf_op jit(solution)/shard_map/ppermute | solution.py:650
  109.1 38.5 %all-to-all-start.1 = ((bf16[64,16,1024]{2,1,0:T(8,128)(2,1)}), bf16[64,16,1024]{2,1,0:T(8,128)(2,1)}, u32[]{:S(2)}, u32[]{:S(2)}) async-start(bf16[64,16,1024]{2,1,0:T(8,128)(2,1)} %bitcast.10), calls=%async_computation.1 | async-start | bytes 4194304 | tf_op jit(solution)/shard_map/all_to_all | solution.py:652
  117.9 1.6 copy-start.7
  119.5 1.6 copy-start.8
  147.5 4.7 %collective-permute-start.5 = (bf16[512,2304]{1,0:T(8,128)(2,1)}, bf16[512,2304]{1,0:T(8,128)(2,1)S(1)}, u32[]{:S(2)}, u32[]{:S(2)}) collective-permute-start(bf16[512,2304]{1,0:T(8,128)(2,1)} %get-tuple-element.51), channel_id=1, source_target_pairs={{0,1},{1,0},{2,3},{3,2},{4,5},{5,4},{6,7},{7,6},{8,9},{9,8},{10,11... | collective-permute-start | bytes 7077896 | tf_op jit(solution)/shard_map/ppermute | solution.py:664
  147.5 4.2 %collective-permute-start.3 = (f32[1,128]{1,0:T(1,128)S(1)}, f32[1,128]{1,0:T(1,128)S(1)}, u32[]{:S(2)}, u32[]{:S(2)}) collective-permute-start(f32[1,128]{1,0:T(1,128)S(1)} %get-tuple-element.38.refs_0_), channel_id=1, source_target_pairs={{0,1},{1,0},{2,3},{3,2},{4,5},{5,4},{6,7},{7,6},{8,9},{9,8},{10,11... | collective-permute-start | bytes 1544 | tf_op jit(solution)/shard_map/ppermute | solution.py:655
  152.9 1.4 copy-start
  154.4 42.5 %all-to-all-start.2 = ((bf16[64,8,2304]{2,1,0:T(8,128)(2,1)}), bf16[64,8,2304]{2,1,0:T(8,128)(2,1)S(1)}, u32[]{:S(2)}, u32[]{:S(2)}) async-start(bf16[64,8,2304]{2,1,0:T(8,128)(2,1)} %bitcast.17), calls=%async_computation.2 | async-start | bytes 4718592 | tf_op jit(solution)/shard_map/all_to_all | solution.py:668
Sparse Core Ops, SparseCore 0:
  20.3 57.7 all-gather.1

commit v3 on v2

--- a/solution.py
+++ b/solution.py
@@ -509,7 +509,7 @@
             pltpu.SemaphoreType.DMA((3, max(parts, 4))),
             pltpu.SemaphoreType.DMA,
         ],
-        compiler_params=pltpu.CompilerParams(vmem_limit_bytes=VMEM_LIMIT),
+        compiler_params=pltpu.CompilerParams(vmem_limit_bytes=58 * 1024 * 1024),
         cost_estimate=pl.CostEstimate(
             flops=6 * tokens * width * ff, bytes_accessed=30 << 20, transcendentals=tokens * ff
         ),
@@ -649,16 +649,14 @@
 
     pair = pair_sum(keep, lax.ppermute(send, "c", SWAP))
     pair, dsecond = lax.optimization_barrier((pair, dsecond))
-    down_came = lax.all_to_all(
-        pair.reshape(chips, rows_down, width), WIRE, split_axis=0, concat_axis=0, tiled=True
-    )
+    down_sum = pair.reshape(4, 4, 4, rows_down, width)
+    for axis in WIRE:
+        down_sum = lax.psum_scatter(down_sum, axis, scatter_dimension=0, tiled=False)
+        down_sum = down_sum.astype(jnp.float32)
     other_totals = lax.ppermute(totals, "c", SWAP)
     keep, send = backward(
         heads, place, rows, weights, gain_rows, pre, dsecond, norm_one, down, dhead
     )
-    send, down_came = lax.optimization_barrier((send, down_came))
-    grad_down = jnp.sum(down_came.astype(jnp.float32), axis=0)
-
     pair = pair_sum(
         keep,
         lax.ppermute(send, "c", SWAP),
@@ -677,7 +675,7 @@
         jnp.transpose(grad_in),
         grad_one.reshape(-1),
         grad_up,
-        grad_down,
+        down_sum,
         grad_two.reshape(-1),
         grad_head,
         grad_std.reshape(-1),

time: 207 us -> 220 us (1.063)
  waiting for transfers between devices: 68.2 us -> 91.2 us
  starting transfers between devices: 33.6 us -> 23.6 us
  Pallas kernels: 72.1 us -> 76.1 us
  local copies, waits for them, and re-layouts: 12 us -> 8.81 us
    reduce_scatter x0 -> x3, waiting for transfers between devices: none -> 53.5 us  [body(): lax.psum_scatter(down_sum, axis, scatter_dimension=0, tiled=False)]
    all_to_all x1, waiting for transfers between devices: 30 us -> 1.88 us  [body(): lax.all_to_all(pair.reshape(chips, rows_up, -1), WIRE, split_axis=0, conc...]
    all_to_all x1 -> x0, starting transfers between devices: 8.84 us -> none  [body(): lax.all_to_all(pair.reshape(chips, rows_down, width), WIRE, split_axis=0,...]
    unnamed x31 -> x37, local copies, waits for them, and re-layouts: 11.4 us -> 8.19 us
    reduce_sum x1 -> x0, other arithmetic: 2.58 us -> none  [body(): grad_down = jnp.sum(down_came.astype(jnp.float32), axis=0)]
    pallas_call x1, Pallas kernels: 26.2 us -> 28.7 us  [backward(): pl.pallas_call(lambda *refs: backward_kernel(heads, parts, *refs), out_sh...]
    convert_element_type x0 -> x1, other arithmetic: none -> 2.31 us  [body(): down_sum = down_sum.astype(jnp.float32)]
  transfers between devices with their start and end apart: 10 -> 12, of which waited for: 10 -> 11; matrix products, arithmetic and copies ran while one was open for 4% -> 3% of each run, Pallas kernels for 20% -> 22%
where the time goes in v3:
time: 220 us
  waiting for transfers between devices  91.2 us (41%)
  Pallas kernels  76.1 us (35%)
  starting transfers between devices  23.6 us (11%)
  between operations  15.8 us (7%)
  local copies, waits for them, and re-layouts  8.81 us (4%)
  other arithmetic  4.33 us (2%)
    reduce_scatter x3, waiting for transfers between devices, body(): lax.psum_scatter(down_sum, axis, scatter_dimension=0, tiled=False)  53.5 us
    pallas_call x1, Pallas kernels, backward(): pl.pallas_call(lambda *refs: backward_kernel(heads, parts, *refs), out_sh...  28.7 us
    pallas_call x1, Pallas kernels, forward(): pl.pallas_call(lambda *refs: forward_kernel(acts, factor, parts, *refs),...  24.8 us
    pallas_call x1, Pallas kernels, rollout(): pl.pallas_call(rollout_kernel, out_shape=(jax.ShapeDtypeStruct((dof, envs...  15.8 us
    all_gather x1, waiting for transfers between devices, body(): weights = lax.all_gather(ordered, ('z', 'y', 'c'), axis=0, tiled=True)  15.4 us
    all_to_all x1, waiting for transfers between devices, body(): lax.all_to_all(picked.reshape(count, per_peer, row_width), EVERY, split_a...  9.29 us
    all_to_all x1, starting transfers between devices, body(): lax.all_to_all(picked.reshape(count, per_peer, row_width), EVERY, split_a...  9.24 us
    all_to_all x1, starting transfers between devices, body(): lax.all_to_all(pair.reshape(chips, rows_up, -1), WIRE, split_axis=0, conc...  8.24 us
  transfers between devices with their start and end apart: 12, of which 11 were waited for; matrix products, arithmetic and copies ran while one was open for 3% of the time, Pallas kernels for 22%

profile of v3, /device:TPU:0, one launch (start us, length us, event | category | flops | bytes accessed | tf_op | source)
XLA Modules:
  0.0 219.7 jit_solution(16205844960132272477)
XLA Ops:
  7.3 1.6 pack.1
  8.9 2.8 %collective-permute-start = (bf16[8,4352]{1,0:T(8,128)(2,1)}, bf16[8,4352]{1,0:T(8,128)(2,1)S(1)}, u32[]{:S(2)}, u32[]{:S(2)}) collective-permute-start(bf16[8,4352]{1,0:T(8,128)(2,1)} %pack.1), channel_id=1, source_target_pairs={{32,0},{64,32},{96,64},{0,96},{33,1},{65,33},{97,65},{1,97},{34,2}... | collective-permute-start | bytes 208904 | tf_op jit(solution)/shard_map/ppermute | solution.py:629
  11.7 0.8 collective-permute-start.1
  12.5 0.9 collective-permute-start.2
  13.4 0.9 collective-permute-done
  14.3 3.5 %collective-permute-done.1 = bf16[8,4352]{1,0:T(8,128)(2,1)S(1)} collective-permute-done((bf16[8,4352]{1,0:T(8,128)(2,1)}, bf16[8,4352]{1,0:T(8,128)(2,1)S(1)}, u32[]{:S(2)}, u32[]{:S(2)}) %collective-permute-start.1) | collective-permute-done | bytes 69664 | tf_op jit(solution)/shard_map/ppermute | solution.py:629
  18.6 1.6 pad_maximum_fusion
  20.2 1.1 copy.35.geom_ref
  21.3 0.9 copy.36.act_ref
  22.2 0.8 copy.34
  23.1 0.8 copy.37.map_ref
  23.9 0.8 copy-done.4
  24.7 0.7 copy-done.5
  25.4 0.7 copy-done.6
  26.1 0.7 copy-done.7
  26.8 15.8 %rollout.1 = (f32[30,128]{1,0:T(8,128)}, f32[30,128]{1,0:T(8,128)}, bf16[1024,128]{1,0:T(8,128)(2,1)}) custom-call(f32[30,128]{1,0:T(8,128)S(1)} %copy-done.6, f32[30,128]{1,0:T(8,128)S(1)} %copy-done.7, f32[30,30,128]{2,1,0:T(8,128)S(1)} %copy-done.2, f32[24,30,128]{2,1,0:T(8,128)S(1)} %copy.35.geom_ref, s32[2,48,128]{2,1,0:T(8,128)S(1)} %copy-done.4, ...), custom_call_target="tpu_custom_call" | custom-call | tf_op jit(solution)/shard_map/rollout/pallas_call | solution.py:134
  42.7 9.2 %all-to-all-start = ((bf16[128,8,128]{2,1,0:T(8,128)(2,1)}), bf16[128,8,128]{2,1,0:T(8,128)(2,1)S(1)}, u32[]{:S(2)}, u32[]{:S(2)}) async-start(bf16[128,8,128]{2,1,0:T(8,128)(2,1)} %bitcast.2), calls=%async_computation | async-start | bytes 524288 | tf_op jit(solution)/shard_map/all_to_all | solution.py:638
  53.4 9.3 %all-to-all-done = bf16[128,8,128]{2,1,0:T(8,128)(2,1)S(1)} async-done(((bf16[128,8,128]{2,1,0:T(8,128)(2,1)}), bf16[128,8,128]{2,1,0:T(8,128)(2,1)S(1)}, u32[]{:S(2)}, u32[]{:S(2)}) %all-to-all-start) | async-done | bytes 262176 | tf_op jit(solution)/shard_map/all_to_all | solution.py:638
  62.7 15.4 %all-gather.2.cloned.1.call-done.refs_4_.refs_2_ = bf16[256,17408]{1,0:T(8,128)(2,1)} async-done(((bf16[8,17408]{1,0:T(8,128)(2,1)}), bf16[256,17408]{1,0:T(8,128)(2,1)}) %all-gather.2.cloned.1.call-update) | async-done | bytes 8912912 | tf_op jit(solution)/shard_map/all_gather | solution.py:631
  78.1 24.8 %forward.1 = (bf16[1024,1024]{1,0:T(8,128)(2,1)S(1)}, bf16[1024,1024]{1,0:T(8,128)(2,1)S(1)}, bf16[1024,2048]{1,0:T(8,128)(2,1)}, bf16[1024,1024]{1,0:T(8,128)(2...) custom-call(s32[2]{0:T(128)S(1)} %pad_add_fusion.refs_0_, ...), custom_call_target="tpu_custom_call" | custom-call | flops 12884901888 | bytes 31457280 | tf_op jit(solution)/shard_map/forward/pallas_call | solution.py:378
  103.3 3.9 %collective-permute-done.4.came_ref = bf16[1024,1024]{1,0:T(8,128)(2,1)S(1)} collective-permute-done((bf16[1024,1024]{1,0:T(8,128)(2,1)S(1)}, bf16[1024,1024]{1,0:T(8,128)(2,1)S(1)}, u32[]{:S(2)}, u32[]{:S(2)}) %collective-permute-start.4) | collective-permute-done | bytes 2097184 | tf_op jit(solution)/shard_map/ppermute | solution.py:650
  107.2 1.8 pair.2
  109.3 28.7 %backward.1 = (bf16[512,2304]{1,0:T(8,128)(2,1)}, bf16[512,2304]{1,0:T(8,128)(2,1)}) custom-call(s32[2]{0:T(128)} %copy-done.8, bf16[1024,128]{1,0:T(8,128)(2,1)} %bitcast.24, bf16[256,17408]{1,0:T(8,128)(2,1)} %all-gather.2.cloned.1.call-done.refs_4_.refs_2_, f32[8,1024]{1,0:T(8,128)} %copy-done.11, bf16[1024,2048]{1,0:T(8,128)(2,1)} %get-tuple-element.38.refs_4_, ...), custom_call_target="tpu_custom_call" | custom-call | flops 12884901888 | bytes 31457280 | tf_op jit(solution)/shard_map/backward/pallas_call | solution.py:493
  138.3 2.3 %bitcast_convert_fusion = f32[4,4,16,1024]{3,2,1,0:T(8,128)} fusion(bf16[1,4,4,16,1024]{4,3,2,1,0:T(8,128)(2,1)} %reduce-scatter.4.cloned.1.call-done), kind=kLoop, calls=%fused_computation.1 | loop fusion | flops 262144 | bytes 1572864 | tf_op jit(solution)/shard_map/convert_element_type | solution.py:655
  141.0 1.6 collective-permute-done.3.refs_1_
  143.0 2.3 %pair.3 = bf16[512,2304]{1,0:T(8,128)(2,1)S(1)} custom-call(f32[1,128]{1,0:T(1,128)S(1)} %get-tuple-element.36.refs_0_, f32[1,128]{1,0:T(1,128)S(1)} %collective-permute-done.3.refs_1_, bf16[512,2304]{1,0:T(8,128)(2,1)S(1)} %copy-done.1, bf16[512,2304]{1,0:T(8,128)(2,1)} %collective-permute-done.5.refs_3_), custom_call_target="tpu_custom_call" | custom-call | tf_op jit(solution)/shard_map/pair/pallas_call | solution.py:553
  145.3 1.4 copy-done
  146.7 8.2 %all-to-all-start.1 = ((bf16[64,8,2304]{2,1,0:T(8,128)(2,1)}), bf16[64,8,2304]{2,1,0:T(8,128)(2,1)S(1)}, u32[]{:S(2)}, u32[]{:S(2)}) async-start(bf16[64,8,2304]{2,1,0:T(8,128)(2,1)} %bitcast.22), calls=%async_computation.1 | async-start | bytes 4718592 | tf_op jit(solution)/shard_map/all_to_all | solution.py:666
  155.0 30.8 %reduce-scatter.6.cloned.1.call-done = f32[1,4,16,1024]{3,2,1,0:T(8,128)} async-done(((f32[4,4,16,1024]{3,2,1,0:T(8,128)}), f32[1,4,16,1024]{3,2,1,0:T(8,128)}) %reduce-scatter.6.cloned.1.call-update) | async-done | bytes 262160 | tf_op jit(solution)/shard_map/reduce_scatter | solution.py:654
  185.8 1.9 all-to-all-done.1.refs_0_
  187.7 1.0 finish.1
  189.3 22.7 %reduce-scatter.8.cloned.1.call-done = f32[1,16,1024]{2,1,0:T(8,128)} async-done(((f32[4,16,1024]{2,1,0:T(8,128)}), f32[1,16,1024]{2,1,0:T(8,128)}) %reduce-scatter.8.cloned.1.call-update) | async-done | bytes 65552 | tf_op jit(solution)/shard_map/reduce_scatter | solution.py:654
  (50 shorter events, 4.0 us)
Async XLA Ops:
  7.2 16.7 %copy-start.2 = (f32[30,30,128]{2,1,0:T(8,128)S(1)}, f32[30,30,128]{2,1,0:T(8,128)}, u32[]{:S(2)}) copy-start(f32[30,30,128]{2,1,0:T(8,128)} %minv_ref.1) | copy-start | bytes 1382404
  7.2 45.0 %copy-start.12 = (f32[1024,20]{0,1:T(8,128)S(1)}, f32[1024,20]{0,1:T(8,128)}, u32[]{:S(2)}) copy-start(f32[1024,20]{0,1:T(8,128)} %param.35) | copy-start | bytes 245764
  7.2 45.2 %copy-start.13 = (f32[1024]{0:T(1024)S(1)}, f32[1024]{0:T(1024)}, u32[]{:S(2)}) copy-start(f32[1024]{0:T(1024)} %param.36) | copy-start | bytes 12292
  7.2 70.8 %all-gather.2.cloned.1.call-start = ((), (), s32[]{:S(2)}) async-start(), calls=%async_computation.5 | async-start | bytes 9191424 | tf_op jit(solution)/shard_map/all_gather | solution.py:631
  8.9 43.8 %copy-start.14 = (f32[1024]{0:T(1024)S(1)}, f32[1024]{0:T(1024)}, u32[]{:S(2)}) copy-start(f32[1024]{0:T(1024)} %param.37) | copy-start | bytes 12292
  8.9 5.5 %collective-permute-start = (bf16[8,4352]{1,0:T(8,128)(2,1)}, bf16[8,4352]{1,0:T(8,128)(2,1)S(1)}, u32[]{:S(2)}, u32[]{:S(2)}) collective-permute-start(bf16[8,4352]{1,0:T(8,128)(2,1)} %pack.1), channel_id=1, source_target_pairs={{32,0},{64,32},{96,64},{0,96},{33,1},{65,33},{97,65},{1,97},{34,2}... | collective-permute-start | bytes 208904 | tf_op jit(solution)/shard_map/ppermute | solution.py:629
  11.7 6.1 %collective-permute-start.1 = (bf16[8,4352]{1,0:T(8,128)(2,1)}, bf16[8,4352]{1,0:T(8,128)(2,1)S(1)}, u32[]{:S(2)}, u32[]{:S(2)}) collective-permute-start(bf16[8,4352]{1,0:T(8,128)(2,1)} %pack.1), channel_id=1, source_target_pairs={{64,0},{96,32},{0,64},{32,96},{65,1},{97,33},{1,65},{33,97},{66,2}... | collective-permute-start | bytes 208904 | tf_op jit(solution)/shard_map/ppermute | solution.py:629
  12.5 6.0 %collective-permute-start.2 = (bf16[8,4352]{1,0:T(8,128)(2,1)}, bf16[8,4352]{1,0:T(8,128)(2,1)S(1)}, u32[]{:S(2)}, u32[]{:S(2)}) collective-permute-start(bf16[8,4352]{1,0:T(8,128)(2,1)} %pack.1), channel_id=1, source_target_pairs={{96,0},{0,32},{32,64},{64,96},{97,1},{1,33},{33,65},{65,97},{98,2}... | collective-permute-start | bytes 208904 | tf_op jit(solution)/shard_map/ppermute | solution.py:629
  20.2 32.8 %copy-start.15 = (f32[20]{0:T(128)S(1)}, f32[20]{0:T(128)}, u32[]{:S(2)}) copy-start(f32[20]{0:T(128)} %param.34) | copy-start | bytes 244
  23.9 0.8 copy-start.4
  24.7 0.7 copy-start.5
  25.4 0.7 copy-start.6
  26.1 0.7 copy-start.7
  42.7 20.0 %all-to-all-start = ((bf16[128,8,128]{2,1,0:T(8,128)(2,1)}), bf16[128,8,128]{2,1,0:T(8,128)(2,1)S(1)}, u32[]{:S(2)}, u32[]{:S(2)}) async-start(bf16[128,8,128]{2,1,0:T(8,128)(2,1)} %bitcast.2), calls=%async_computation | async-start | bytes 524288 | tf_op jit(solution)/shard_map/all_to_all | solution.py:638
  51.9 86.4 %reduce-scatter.4.cloned.1.call-start = ((), (), s32[]{:S(2)}) async-start(), calls=%async_computation.6 | async-start | bytes 2621440 | tf_op jit(solution)/shard_map/reduce_scatter | solution.py:654
  52.2 50.7 %copy-start.8 = (s32[2]{0:T(128)}, s32[2]{0:T(128)S(1)}, u32[]{:S(2)}) copy-start(s32[2]{0:T(128)S(1)} %pad_add_fusion.refs_0_) | copy-start | bytes 28
  62.7 40.2 %copy-start.3 = (bf16[128,8,128]{2,1,0:T(8,128)(2,1)}, bf16[128,8,128]{2,1,0:T(8,128)(2,1)S(1)}, u32[]{:S(2)}) copy-start(bf16[128,8,128]{2,1,0:T(8,128)(2,1)S(1)} %all-to-all-done) | copy-start | bytes 786436
  102.9 6.1 %copy-start.9 = (bf16[1024,1024]{1,0:T(8,128)(2,1)}, bf16[1024,1024]{1,0:T(8,128)(2,1)S(1)}, u32[]{:S(2)}) copy-start(bf16[1024,1024]{1,0:T(8,128)(2,1)S(1)} %get-tuple-element.42.refs_5_) | copy-start | bytes 6291460
  102.9 6.1 %copy-start.10 = (f32[136,1024]{1,0:T(8,128)}, f32[136,1024]{1,0:T(8,128)S(1)}, u32[]{:S(2)}) copy-start(f32[136,1024]{1,0:T(8,128)S(1)} %get-tuple-element.45.refs_8_) | copy-start | bytes 1671172
  102.9 6.1 %copy-start.11 = (f32[8,1024]{1,0:T(8,128)}, f32[8,1024]{1,0:T(8,128)S(1)}, u32[]{:S(2)}) copy-start(f32[8,1024]{1,0:T(8,128)S(1)} %get-tuple-element.37.refs_3_) | copy-start | bytes 98308
  102.9 4.2 %collective-permute-start.4 = (bf16[1024,1024]{1,0:T(8,128)(2,1)S(1)}, bf16[1024,1024]{1,0:T(8,128)(2,1)S(1)}, u32[]{:S(2)}, u32[]{:S(2)}) collective-permute-start(bf16[1024,1024]{1,0:T(8,128)(2,1)S(1)} %get-tuple-element.40), channel_id=1, source_target_pairs={{0,1},{1,0},{2,3},{3,2},{4,5},{5,4},{6,7},{7,6},{8,9},{9,8},{10,11... | collective-permute-start | bytes 6291464 | tf_op jit(solution)/shard_map/ppermute | solution.py:650
  109.0 76.8 %reduce-scatter.6.cloned.1.call-start = ((), (), s32[]{:S(2)}) async-start(), calls=%async_computation.7 | async-start | bytes 1310720 | tf_op jit(solution)/shard_map/reduce_scatter | solution.py:654
  138.0 5.0 %copy-start.1 = (bf16[512,2304]{1,0:T(8,128)(2,1)S(1)}, bf16[512,2304]{1,0:T(8,128)(2,1)}, u32[]{:S(2)}) copy-start(bf16[512,2304]{1,0:T(8,128)(2,1)} %get-tuple-element.46.refs_2_) | copy-start | bytes 7077892
  138.0 5.0 %collective-permute-start.5 = (bf16[512,2304]{1,0:T(8,128)(2,1)}, bf16[512,2304]{1,0:T(8,128)(2,1)}, u32[]{:S(2)}, u32[]{:S(2)}) collective-permute-start(bf16[512,2304]{1,0:T(8,128)(2,1)} %get-tuple-element.47), channel_id=1, source_target_pairs={{0,1},{1,0},{2,3},{3,2},{4,5},{5,4},{6,7},{7,6},{8,9},{9,8},{10,11... | collective-permute-start | bytes 7077896 | tf_op jit(solution)/shard_map/ppermute | solution.py:662
  140.7 1.9 collective-permute-start.3
  145.3 1.4 copy-start
  146.7 41.0 %all-to-all-start.1 = ((bf16[64,8,2304]{2,1,0:T(8,128)(2,1)}), bf16[64,8,2304]{2,1,0:T(8,128)(2,1)S(1)}, u32[]{:S(2)}, u32[]{:S(2)}) async-start(bf16[64,8,2304]{2,1,0:T(8,128)(2,1)} %bitcast.22), calls=%async_computation.1 | async-start | bytes 4718592 | tf_op jit(solution)/shard_map/all_to_all | solution.py:666
  154.9 57.1 %reduce-scatter.8.cloned.1.call-start = ((), (), s32[]{:S(2)}) async-start(), calls=%async_computation.8 | async-start | bytes 327680 | tf_op jit(solution)/shard_map/reduce_scatter | solution.py:654
Sparse Core Ops, SparseCore 0:
  20.3 57.7 all-gather.1
  109.2 28.8 reduce-scatter.3
  140.8 44.9 reduce-scatter.5
  188.6 23.4 reduce-scatter.7

commit v4 on v2

--- a/solution.py
+++ b/solution.py
@@ -406,27 +406,19 @@
     )(place, rows, aux, std, weights)
 
 
-def backward_kernel(
-    heads, parts,
-    place_ref, rows_ref, weights_ref, gains_ref, pre_hbm, dsecond_hbm, norm_hbm, down_hbm, dhead_ref,
-    keep_ref, send_hbm,
-    up_ref, win_ref, down_ref, pre_ref, dsecond_ref, norm_ref, dpre_ref, din_ref, dgain_ref, send_ref,
-    in_sem, out_sem,
+def backward_up_kernel(
+    place_ref, pre_hbm, dsecond_hbm, norm_hbm, down_hbm, dpre_ref, keep_ref, send_hbm,
+    pre_ref, dsecond_ref, norm_ref, down_ref, send_ref, in_sem, out_sem,
 ):
-    tokens = rows_ref.shape[0]
-    width, ff = up_ref.shape
-    load_win = columns_in(weights_ref, parts, place_ref[1], ff + 2 * width, win_ref, in_sem.at[0])
-    load_up = columns_in(weights_ref, parts, place_ref[1], 0, up_ref, in_sem.at[1])
+    tokens, ff = pre_ref.shape
+    width = norm_ref.shape[1]
     pairs = ((dsecond_hbm, dsecond_ref), (down_hbm, down_ref), (pre_hbm, pre_ref), (norm_hbm, norm_ref))
     loads = [
-        pltpu.make_async_copy(there, here, in_sem.at[2, place])
-        for place, (there, here) in enumerate(pairs)
+        pltpu.make_async_copy(there, here, in_sem.at[which])
+        for which, (there, here) in enumerate(pairs)
     ]
-    for copy in loads[:3] + load_win + load_up + loads[3:]:
+    for copy in loads:
         copy.start()
-    gain_one = gains_ref[0:1, :]
-    din_ref[...] = jnp.zeros_like(din_ref)
-    dgain_ref[...] = jnp.zeros_like(dgain_ref)
     for copy in loads[:3]:
         copy.wait()
 
@@ -447,6 +439,64 @@
             )
             dpre_ref[at, lanes] = (dhidden * slope).astype(jnp.bfloat16)
 
+    loads[3].wait()
+    chunk = 512
+
+    @pl.loop(0, width // chunk)
+    def _(block):
+        lanes = pl.ds(pl.multiple_of(block * chunk, chunk), chunk)
+        half = block * (chunk // 2)
+        for start in range(0, ff, 1024):
+            grad = dot(norm_ref[:, lanes], dpre_ref[:, start : start + 1024], TN)
+            split_by_core(place_ref[0], grad, 8, keep_ref, send_ref, half, start)
+        at = pl.ds(pl.multiple_of(half, chunk // 2), chunk // 2)
+        pltpu.make_async_copy(send_ref.at[at, :], send_hbm.at[at, :], out_sem).start()
+
+    pltpu.make_async_copy(send_ref, send_hbm, out_sem).wait()
+
+
+def backward_up(place, pre, dsecond, norm_one, down):
+    tokens, ff = pre.shape
+    width = dsecond.shape[1]
+    bf16 = jnp.bfloat16
+    out = jax.ShapeDtypeStruct((width // 2, ff), bf16)
+    return pl.pallas_call(
+        backward_up_kernel,
+        out_shape=(jax.ShapeDtypeStruct((tokens, ff), bf16), out, out),
+        in_specs=[SMEM] + [HBM] * 4,
+        out_specs=(VMEM, VMEM, HBM),
+        scratch_shapes=[
+            pltpu.VMEM((tokens, ff), bf16),
+            pltpu.VMEM((tokens, width), bf16),
+            pltpu.VMEM((tokens, width), bf16),
+            pltpu.VMEM((ff, width), bf16),
+            pltpu.VMEM(out.shape, bf16),
+            pltpu.SemaphoreType.DMA((4,)),
+            pltpu.SemaphoreType.DMA,
+        ],
+        compiler_params=pltpu.CompilerParams(vmem_limit_bytes=VMEM_LIMIT),
+        cost_estimate=pl.CostEstimate(
+            flops=4 * tokens * width * ff, bytes_accessed=20 << 20, transcendentals=tokens * ff
+        ),
+        name="backward_up",
+    )(place, pre, dsecond, norm_one, down)
+
+
+def backward_in_kernel(
+    heads, parts,
+    place_ref, rows_ref, weights_ref, gains_ref, dpre_ref, dsecond_ref, dhead_ref,
+    keep_ref, send_ref,
+    up_ref, win_ref, din_ref, dgain_ref, in_sem,
+):
+    tokens = rows_ref.shape[0]
+    width, ff = up_ref.shape
+    load_win = columns_in(weights_ref, parts, place_ref[1], ff + 2 * width, win_ref, in_sem.at[0])
+    load_up = columns_in(weights_ref, parts, place_ref[1], 0, up_ref, in_sem.at[1])
+    for copy in load_win + load_up:
+        copy.start()
+    gain_one = gains_ref[0:1, :]
+    din_ref[...] = jnp.zeros_like(din_ref)
+    dgain_ref[...] = jnp.zeros_like(dgain_ref)
     for copy in load_win + load_up:
         copy.wait()
 
@@ -462,59 +512,44 @@
         dfirst = dfirst + norm_backward(dnorm * gain_one, first, root)
         din_ref[...] += dot(rows, dfirst.astype(jnp.bfloat16), TN)
 
-    loads[3].wait()
     chunk = 512
     ids = lax.broadcasted_iota(jnp.int32, (LANES, chunk), 0)
 
     @pl.loop(0, width // chunk)
     def _(block):
         lanes = pl.ds(pl.multiple_of(block * chunk, chunk), chunk)
+        half = block * (chunk // 2)
         core = place_ref[0]
-        half = block * (chunk // 2)
-        for start in range(0, ff, 1024):
-            grad = dot(norm_ref[:, lanes], dpre_ref[:, start : start + 1024], TN)
-            split_by_core(core, grad, 8, keep_ref, send_ref, half, start)
-        split_by_core(core, jnp.transpose(din_ref[:, lanes]), 8, keep_ref, send_ref, half, ff)
+        split_by_core(core, jnp.transpose(din_ref[:, lanes]), 8, keep_ref, send_ref, half, 0)
         tail = jnp.where(ids == heads, dgain_ref[0:1, lanes], dhead_ref[0:LANES, lanes])
         tail = jnp.where(ids == heads + 1, dhead_ref[LANES : LANES + 1, lanes], tail)
-        split_by_core(core, jnp.transpose(tail), 8, keep_ref, send_ref, half, ff + LANES)
-        at = pl.ds(pl.multiple_of(half, chunk // 2), chunk // 2)
-        pltpu.make_async_copy(send_ref.at[at, :], send_hbm.at[at, :], out_sem).start()
-
-    pltpu.make_async_copy(send_ref, send_hbm, out_sem).wait()
-
-
-def backward(heads, place, rows, weights, gains, pre, dsecond, norm_one, down, dhead):
-    tokens, ff = pre.shape
+        split_by_core(core, jnp.transpose(tail), 8, keep_ref, send_ref, half, LANES)
+
+
+def backward_in(heads, place, rows, weights, gains, dpre, dsecond, dhead):
+    tokens, ff = dpre.shape
     width = dsecond.shape[1]
     parts = width // weights.shape[0]
     bf16, f32 = jnp.bfloat16, jnp.float32
-    out = jax.ShapeDtypeStruct((width // 2, ff + 2 * LANES), bf16)
+    out = jax.ShapeDtypeStruct((width // 2, 2 * LANES), bf16)
     return pl.pallas_call(
-        lambda *refs: backward_kernel(heads, parts, *refs),
+        lambda *refs: backward_in_kernel(heads, parts, *refs),
         out_shape=(out, out),
-        in_specs=[SMEM, VMEM, HBM, VMEM] + [HBM] * 4 + [VMEM],
-        out_specs=(VMEM, HBM),
+        in_specs=[SMEM, VMEM, HBM] + [VMEM] * 4,
+        out_specs=(VMEM, VMEM),
         scratch_shapes=[
             pltpu.VMEM((width, ff), bf16),
             pltpu.VMEM((width, LANES), bf16),
-            pltpu.VMEM((ff, width), bf16),
-            pltpu.VMEM((tokens, ff), bf16),
-            pltpu.VMEM((tokens, width), bf16),
-            pltpu.VMEM((tokens, width), bf16),
-            pltpu.VMEM((tokens, ff), bf16),
             pltpu.VMEM((LANES, width), f32),
             pltpu.VMEM((8, width), f32),
-            pltpu.VMEM(out.shape, bf16),
-            pltpu.SemaphoreType.DMA((3, max(parts, 4))),
-            pltpu.SemaphoreType.DMA,
+            pltpu.SemaphoreType.DMA((2, parts)),
         ],
         compiler_params=pltpu.CompilerParams(vmem_limit_bytes=VMEM_LIMIT),
         cost_estimate=pl.CostEstimate(
-            flops=6 * tokens * width * ff, bytes_accessed=30 << 20, transcendentals=tokens * ff
+            flops=2 * tokens * width * ff, bytes_accessed=12 << 20, transcendentals=0
         ),
-        name="backward",
-    )(place, rows, weights, gains, pre, dsecond, norm_one, down, dhead)
+        name="backward_in",
+    )(place, rows, weights, gains, dpre, dsecond, dhead)
 
 
 def pair_kernel(keep_ref, came_ref, out_ref):
@@ -527,10 +562,12 @@
         out_ref[at, :] = total.astype(jnp.bfloat16)
 
 
-def pair_totals_kernel(place, count, rows, mine_ref, other_ref, keep_ref, came_ref, out_ref):
+def pair_totals_kernel(place, count, rows, mine_ref, other_ref, keep_in, came_in, keep_ref, came_ref, out_ref):
     f32, bf16 = jnp.float32, jnp.bfloat16
-    cut = keep_ref.shape[1] - LANES
-    pair_kernel(keep_ref.at[:, :cut], came_ref.at[:, :cut], out_ref.at[:, :cut])
+    ff = keep_ref.shape[1]
+    cut = ff + LANES
+    pair_kernel(keep_ref, came_ref, out_ref.at[:, :ff])
+    pair_kernel(keep_in.at[:, :LANES], came_in.at[:, :LANES], out_ref.at[:, ff:cut])
     lane = lax.broadcasted_iota(jnp.int32, (8, LANES), 1)
     totals = jnp.broadcast_to(mine_ref[...] + other_ref[...], (8, LANES))
     totals = jnp.where(lane < count, totals, 0.0)
@@ -542,17 +579,17 @@
         + pltpu.roll(second, place + count, 1)
         + pltpu.roll(third, place + 2 * count, 1)
     )
-    tail = keep_ref[:, cut:].astype(f32) + came_ref[:, cut:].astype(f32)
+    tail = keep_in[:, LANES:].astype(f32) + came_in[:, LANES:].astype(f32)
     row = lax.broadcasted_iota(jnp.int32, tail.shape, 0) % rows
     lane = lax.broadcasted_iota(jnp.int32, tail.shape, 1)
     special = (row == 0) & (lane >= place) & (lane < place + 3 * count)
     out_ref[:, cut:] = jnp.where(special, line[0:1], tail).astype(bf16)
 
 
-def pair_sum(keep, came, kernel=pair_kernel, small=()):
+def pair_sum(keep, came, kernel=pair_kernel, small=(), more=0):
     return pl.pallas_call(
         kernel,
-        out_shape=jax.ShapeDtypeStruct(keep.shape, keep.dtype),
+        out_shape=jax.ShapeDtypeStruct((keep.shape[0], keep.shape[1] + more), keep.dtype),
         in_specs=[VMEM] * (len(small) + 2),
         out_specs=VMEM,
         compiler_params=pltpu.CompilerParams(vmem_limit_bytes=VMEM_LIMIT // 3),
@@ -653,17 +690,19 @@
         pair.reshape(chips, rows_down, width), WIRE, split_axis=0, concat_axis=0, tiled=True
     )
     other_totals = lax.ppermute(totals, "c", SWAP)
-    keep, send = backward(
-        heads, place, rows, weights, gain_rows, pre, dsecond, norm_one, down, dhead
-    )
-    send, down_came = lax.optimization_barrier((send, down_came))
+    dpre, keep, send = backward_up(place, pre, dsecond, norm_one, down)
+    came = lax.ppermute(send, "c", SWAP)
+    keep_in, send_in = backward_in(
+        heads, place, rows, weights, gain_rows, dpre, dsecond, dhead
+    )
+    send_in, down_came = lax.optimization_barrier((send_in, down_came))
     grad_down = jnp.sum(down_came.astype(jnp.float32), axis=0)
-
     pair = pair_sum(
         keep,
-        lax.ppermute(send, "c", SWAP),
+        came,
         lambda *refs: pair_totals_kernel(heads + 2, acts + 1, rows_up, *refs),
-        (totals, other_totals),
+        (totals, other_totals, keep_in, lax.ppermute(send_in, "c", SWAP)),
+        2 * LANES,
     )
     up_came = lax.all_to_all(
         pair.reshape(chips, rows_up, -1), WIRE, split_axis=0, concat_axis=0, tiled=True

time: 207 us -> 211 us (1.019)
  Pallas kernels: 72.1 us -> 78.5 us
    pallas_call x3 -> x4, Pallas kernels: 28.7 us -> 35.2 us  [the longest x1 20.8 us: backward_up(): pl.pallas_call(backward_up_kernel, out_shape=(jax.ShapeDtypeStruct((token...]
    ppermute x1, waiting for transfers between devices: 3.65 us -> 1.07 us  [body(): other_totals = lax.ppermute(totals, 'c', SWAP)]
  transfers between devices with their start and end apart: 10 -> 11, of which waited for: 10 -> 8; matrix products, arithmetic and copies ran while one was open for 4% -> 4% of each run, Pallas kernels for 20% -> 22%
where the time goes in v4:
time: 211 us; the launch traced here: 210 us
  Pallas kernels  78.5 us (37%)
  waiting for transfers between devices  67 us (32%)
  starting transfers between devices  32.4 us (15%)
  between operations  16 us (8%)
  local copies, waits for them, and re-layouts  11 us (5%)
  other arithmetic  4.61 us (2%)
    all_to_all x1, waiting for transfers between devices, body(): lax.all_to_all(pair.reshape(chips, rows_up, -1), WIRE, split_axis=0, conc...  30.2 us
    pallas_call x1, Pallas kernels, forward(): pl.pallas_call(lambda *refs: forward_kernel(acts, factor, parts, *refs),...  24.8 us
    pallas_call x1, Pallas kernels, backward_up(): pl.pallas_call(backward_up_kernel, out_shape=(jax.ShapeDtypeStruct((token...  20.8 us
    all_gather x1, waiting for transfers between devices, body(): weights = lax.all_gather(ordered, ('z', 'y', 'c'), axis=0, tiled=True)  17.3 us
    pallas_call x1, Pallas kernels, rollout(): pl.pallas_call(rollout_kernel, out_shape=(jax.ShapeDtypeStruct((dof, envs...  15.9 us
    pallas_call x1, Pallas kernels, backward_in(): pl.pallas_call(lambda *refs: backward_in_kernel(heads, parts, *refs), out...  10.3 us
    unnamed x31, local copies, waits for them, and re-layouts  10.3 us
    all_to_all x1, starting transfers between devices, body(): lax.all_to_all(pair.reshape(chips, rows_up, -1), WIRE, split_axis=0, conc...  10.1 us
  transfers between devices with their start and end apart: 11, of which 8 were waited for; matrix products, arithmetic and copies ran while one was open for 4% of the time, Pallas kernels for 22%

profile of v4, /device:TPU:0, one launch (start us, length us, event | category | flops | bytes accessed | tf_op | source)
XLA Modules:
  0.0 209.5 jit_solution(18166070091235396238)
XLA Ops:
  7.3 1.6 pack.1
  8.9 2.8 %collective-permute-start = (bf16[8,4352]{1,0:T(8,128)(2,1)}, bf16[8,4352]{1,0:T(8,128)(2,1)S(1)}, u32[]{:S(2)}, u32[]{:S(2)}) collective-permute-start(bf16[8,4352]{1,0:T(8,128)(2,1)} %pack.1), channel_id=1, source_target_pairs={{32,0},{64,32},{96,64},{0,96},{33,1},{65,33},{97,65},{1,97},{34,2}... | collective-permute-start | bytes 208904 | tf_op jit(solution)/shard_map/ppermute | solution.py:666
  11.8 0.8 collective-permute-start.1
  12.6 0.9 collective-permute-start.2
  13.4 0.9 collective-permute-done
  14.4 3.5 %collective-permute-done.1 = bf16[8,4352]{1,0:T(8,128)(2,1)S(1)} collective-permute-done((bf16[8,4352]{1,0:T(8,128)(2,1)}, bf16[8,4352]{1,0:T(8,128)(2,1)S(1)}, u32[]{:S(2)}, u32[]{:S(2)}) %collective-permute-start.1) | collective-permute-done | bytes 69664 | tf_op jit(solution)/shard_map/ppermute | solution.py:666
  17.9 0.7 collective-permute-done.2
  18.6 1.6 pad_maximum_fusion
  20.3 1.1 copy.35.geom_ref
  21.3 0.9 copy.36.act_ref
  22.2 0.8 copy.34
  23.1 0.8 copy.37.map_ref
  24.0 15.9 %rollout.1 = (f32[30,128]{1,0:T(8,128)}, f32[30,128]{1,0:T(8,128)}, bf16[1024,128]{1,0:T(8,128)(2,1)}) custom-call(f32[30,128]{1,0:T(8,128)S(1)} %copy-done.7, f32[30,128]{1,0:T(8,128)S(1)} %copy-done.8, f32[30,30,128]{2,1,0:T(8,128)S(1)} %copy-done.4, f32[24,30,128]{2,1,0:T(8,128)S(1)} %copy.35.geom_ref, s32[2,48,128]{2,1,0:T(8,128)S(1)} %copy-done.5, ...), custom_call_target="tpu_custom_call" | custom-call | tf_op jit(solution)/shard_map/rollout/pallas_call | solution.py:134
  39.8 9.4 %all-to-all-start = ((bf16[128,8,128]{2,1,0:T(8,128)(2,1)}), bf16[128,8,128]{2,1,0:T(8,128)(2,1)S(1)}, u32[]{:S(2)}, u32[]{:S(2)}) async-start(bf16[128,8,128]{2,1,0:T(8,128)(2,1)} %bitcast.2), calls=%async_computation | async-start | bytes 524288 | tf_op jit(solution)/shard_map/all_to_all | solution.py:675
  50.5 9.3 %all-to-all-done = bf16[128,8,128]{2,1,0:T(8,128)(2,1)S(1)} async-done(((bf16[128,8,128]{2,1,0:T(8,128)(2,1)}), bf16[128,8,128]{2,1,0:T(8,128)(2,1)S(1)}, u32[]{:S(2)}, u32[]{:S(2)}) %all-to-all-start) | async-done | bytes 262176 | tf_op jit(solution)/shard_map/all_to_all | solution.py:675
  59.8 17.3 %all-gather.2.cloned.1.call-done.refs_4_.refs_2_ = bf16[256,17408]{1,0:T(8,128)(2,1)} async-done(((bf16[8,17408]{1,0:T(8,128)(2,1)}), bf16[256,17408]{1,0:T(8,128)(2,1)}) %all-gather.2.cloned.1.call-update) | async-done | bytes 8912912 | tf_op jit(solution)/shard_map/all_gather | solution.py:668
  77.1 24.8 %forward.1 = (bf16[1024,1024]{1,0:T(8,128)(2,1)S(1)}, bf16[1024,1024]{1,0:T(8,128)(2,1)S(1)}, bf16[1024,2048]{1,0:T(8,128)(2,1)}, bf16[1024,1024]{1,0:T(8,128)(2...) custom-call(s32[2]{0:T(128)S(1)} %pad_add_fusion.refs_0_.place_ref, ...), custom_call_target="tpu_custom_call" | custom-call | flops 12884901888 | bytes 31457280 | tf_op jit(solution)/shard_map/forward/pallas_call | solution.py:378
  102.3 3.9 %collective-permute-done.4.came_ref = bf16[1024,1024]{1,0:T(8,128)(2,1)S(1)} collective-permute-done((bf16[1024,1024]{1,0:T(8,128)(2,1)S(1)}, bf16[1024,1024]{1,0:T(8,128)(2,1)S(1)}, u32[]{:S(2)}, u32[]{:S(2)}) %collective-permute-start.4) | collective-permute-done | bytes 2097184 | tf_op jit(solution)/shard_map/ppermute | solution.py:687
  106.2 1.9 pair.2
  108.1 7.4 %all-to-all-start.1 = ((bf16[64,16,1024]{2,1,0:T(8,128)(2,1)}), bf16[64,16,1024]{2,1,0:T(8,128)(2,1)}, u32[]{:S(2)}, u32[]{:S(2)}) async-start(bf16[64,16,1024]{2,1,0:T(8,128)(2,1)} %bitcast.10), calls=%async_computation.1 | async-start | bytes 4194304 | tf_op jit(solution)/shard_map/all_to_all | solution.py:689
  115.4 20.8 %backward_up.1 = (bf16[1024,2048]{1,0:T(8,128)(2,1)}, bf16[512,2048]{1,0:T(8,128)(2,1)S(1)}, bf16[512,2048]{1,0:T(8,128)(2,1)}) custom-call(s32[2]{0:T(128)S(1)} %pad_add_fusion.refs_0_.place_ref, bf16[1024,2048]{1,0:T(8,128)(2,1)} %get-tuple-element.43.pre_hbm, bf16[1024,1024]{1,0:T(8,128)(2,1)S(1)} %get-tuple-element.47.dsecond_hbm.refs_5_, ...), custom_call_target="tpu_custom_call" | custom-call | flops 8589934592 | bytes 20971520 | tf_op jit(solution)/shard_map/backward_up/pallas_call | solution.py:463
  136.2 1.3 copy-done.2
  137.5 2.2 %copy-done.1 = bf16[1024,2048]{1,0:T(8,128)(2,1)S(1)} copy-done((bf16[1024,2048]{1,0:T(8,128)(2,1)S(1)}, bf16[1024,2048]{1,0:T(8,128)(2,1)}, u32[]{:S(2)}) %copy-start.1) | copy-done | bytes 4194328
  139.7 10.3 %backward_in.1 = (bf16[512,256]{1,0:T(8,128)(2,1)S(1)}, bf16[512,256]{1,0:T(8,128)(2,1)S(1)}) custom-call(s32[2]{0:T(128)S(1)} %pad_add_fusion.refs_0_.place_ref, bf16[1024,128]{1,0:T(8,128)(2,1)S(1)} %bitcast.19, bf16[256,17408]{1,0:T(8,128)(2,1)} %all-gather.2.cloned.1.call-done.refs_4_.refs_2_, f32[8,1024]{1,0:T(8,128)S(1)} %get-tuple-element.42.refs_3_, ...), custom_call_target="tpu_custom_call" | custom-call | flops 4294967296 | bytes 12582912 | tf_op jit(solution)/shard_map/backward_in/pallas_call | solution.py:535
  150.8 1.1 collective-permute-done.3.refs_1_
  151.8 1.6 copy-done.3
  153.4 2.3 %pair.3 = bf16[512,2304]{1,0:T(8,128)(2,1)S(1)} custom-call(f32[1,128]{1,0:T(1,128)S(1)} %get-tuple-element.41.refs_0_, f32[1,128]{1,0:T(1,128)S(1)} %collective-permute-done.3.refs_1_, bf16[512,256]{1,0:T(8,128)(2,1)S(1)} %get-tuple-element.52.refs_2_, bf16[512,256]{1,0:T(8,128)(2,1)S(1)} %collective-permute-done.5.refs_3_, ...), custom_call_target="tpu_custom_call" | custom-call | tf_op jit(solution)/shard_map/pair/pallas_call | solution.py:590
  155.7 1.4 copy-done
  157.1 10.1 %all-to-all-start.2 = ((bf16[64,8,2304]{2,1,0:T(8,128)(2,1)}), bf16[64,8,2304]{2,1,0:T(8,128)(2,1)S(1)}, u32[]{:S(2)}, u32[]{:S(2)}) async-start(bf16[64,8,2304]{2,1,0:T(8,128)(2,1)} %bitcast.17), calls=%async_computation.2 | async-start | bytes 4718592 | tf_op jit(solution)/shard_map/all_to_all | solution.py:707
  167.2 2.6 %convert_reduce_fusion = f32[16,1024]{1,0:T(8,128)} fusion(bf16[64,16,1024]{2,1,0:T(8,128)(2,1)} %all-to-all-done.1), kind=kLoop, calls=%fused_computation | loop fusion | flops 2080768 | bytes 2162688 | tf_op jit(solution)/shard_map/reduce_sum | solution.py:699
  169.8 30.2 %all-to-all-done.2.refs_0_ = bf16[64,8,2304]{2,1,0:T(8,128)(2,1)S(1)} async-done(((bf16[64,8,2304]{2,1,0:T(8,128)(2,1)}), bf16[64,8,2304]{2,1,0:T(8,128)(2,1)S(1)}, u32[]{:S(2)}, u32[]{:S(2)}) %all-to-all-start.2) | async-done | bytes 2359328 | tf_op jit(solution)/shard_map/all_to_all | solution.py:707
  199.9 1.0 finish.1
  (40 shorter events, 2.4 us)
Async XLA Ops:
  7.2 16.8 %copy-start.7 = (f32[30,128]{1,0:T(8,128)S(1)}, f32[30,128]{1,0:T(8,128)}, u32[]{:S(2)}) copy-start(f32[30,128]{1,0:T(8,128)} %q_ref.1) | copy-start | bytes 46084
  7.2 16.7 %copy-start.8 = (f32[30,128]{1,0:T(8,128)S(1)}, f32[30,128]{1,0:T(8,128)}, u32[]{:S(2)}) copy-start(f32[30,128]{1,0:T(8,128)} %v_ref.1) | copy-start | bytes 46084
  7.2 16.7 %copy-start.4 = (f32[30,30,128]{2,1,0:T(8,128)S(1)}, f32[30,30,128]{2,1,0:T(8,128)}, u32[]{:S(2)}) copy-start(f32[30,30,128]{2,1,0:T(8,128)} %minv_ref.1) | copy-start | bytes 1382404
  7.2 16.7 %copy-start.5 = (s32[2,48,128]{2,1,0:T(8,128)S(1)}, s32[2,48,128]{2,1,0:T(8,128)}, u32[]{:S(2)}) copy-start(s32[2,48,128]{2,1,0:T(8,128)} %pairs_ref.1) | copy-start | bytes 147460
  7.2 16.7 %copy-start.6 = (f32[48,128]{1,0:T(8,128)S(1)}, f32[48,128]{1,0:T(8,128)}, u32[]{:S(2)}) copy-start(f32[48,128]{1,0:T(8,128)} %gap_ref.1) | copy-start | bytes 73732
  7.2 42.1 %copy-start.9 = (f32[1024,20]{0,1:T(8,128)S(1)}, f32[1024,20]{0,1:T(8,128)}, u32[]{:S(2)}) copy-start(f32[1024,20]{0,1:T(8,128)} %param.35) | copy-start | bytes 245764
  7.2 69.9 %all-gather.2.cloned.1.call-start = ((), (), s32[]{:S(2)}) async-start(), calls=%async_computation.3 | async-start | bytes 9191424 | tf_op jit(solution)/shard_map/all_gather | solution.py:668
  8.9 40.6 %copy-start.10 = (f32[1024]{0:T(1024)S(1)}, f32[1024]{0:T(1024)}, u32[]{:S(2)}) copy-start(f32[1024]{0:T(1024)} %param.36) | copy-start | bytes 12292
  8.9 5.5 %collective-permute-start = (bf16[8,4352]{1,0:T(8,128)(2,1)}, bf16[8,4352]{1,0:T(8,128)(2,1)S(1)}, u32[]{:S(2)}, u32[]{:S(2)}) collective-permute-start(bf16[8,4352]{1,0:T(8,128)(2,1)} %pack.1), channel_id=1, source_target_pairs={{32,0},{64,32},{96,64},{0,96},{33,1},{65,33},{97,65},{1,97},{34,2}... | collective-permute-start | bytes 208904 | tf_op jit(solution)/shard_map/ppermute | solution.py:666
  11.8 6.1 %collective-permute-start.1 = (bf16[8,4352]{1,0:T(8,128)(2,1)}, bf16[8,4352]{1,0:T(8,128)(2,1)S(1)}, u32[]{:S(2)}, u32[]{:S(2)}) collective-permute-start(bf16[8,4352]{1,0:T(8,128)(2,1)} %pack.1), channel_id=1, source_target_pairs={{64,0},{96,32},{0,64},{32,96},{65,1},{97,33},{1,65},{33,97},{66,2}... | collective-permute-start | bytes 208904 | tf_op jit(solution)/shard_map/ppermute | solution.py:666
  12.6 6.0 %collective-permute-start.2 = (bf16[8,4352]{1,0:T(8,128)(2,1)}, bf16[8,4352]{1,0:T(8,128)(2,1)S(1)}, u32[]{:S(2)}, u32[]{:S(2)}) collective-permute-start(bf16[8,4352]{1,0:T(8,128)(2,1)} %pack.1), channel_id=1, source_target_pairs={{96,0},{0,32},{32,64},{64,96},{97,1},{1,33},{33,65},{65,97},{98,2}... | collective-permute-start | bytes 208904 | tf_op jit(solution)/shard_map/ppermute | solution.py:666
  20.2 29.6 %copy-start.11 = (f32[1024]{0:T(1024)S(1)}, f32[1024]{0:T(1024)}, u32[]{:S(2)}) copy-start(f32[1024]{0:T(1024)} %param.37) | copy-start | bytes 12292
  20.3 29.8 %copy-start.12 = (f32[20]{0:T(128)S(1)}, f32[20]{0:T(128)}, u32[]{:S(2)}) copy-start(f32[20]{0:T(128)} %param.34) | copy-start | bytes 244
  39.8 20.0 %all-to-all-start = ((bf16[128,8,128]{2,1,0:T(8,128)(2,1)}), bf16[128,8,128]{2,1,0:T(8,128)(2,1)S(1)}, u32[]{:S(2)}, u32[]{:S(2)}) async-start(bf16[128,8,128]{2,1,0:T(8,128)(2,1)} %bitcast.2), calls=%async_computation | async-start | bytes 524288 | tf_op jit(solution)/shard_map/all_to_all | solution.py:675
  101.9 4.2 %collective-permute-start.4 = (bf16[1024,1024]{1,0:T(8,128)(2,1)S(1)}, bf16[1024,1024]{1,0:T(8,128)(2,1)S(1)}, u32[]{:S(2)}, u32[]{:S(2)}) collective-permute-start(bf16[1024,1024]{1,0:T(8,128)(2,1)S(1)} %get-tuple-element.45), channel_id=1, source_target_pairs={{0,1},{1,0},{2,3},{3,2},{4,5},{5,4},{6,7},{7,6},{8,9},{9,8},{10,11... | collective-permute-start | bytes 6291464 | tf_op jit(solution)/shard_map/ppermute | solution.py:687
  108.1 42.0 %all-to-all-start.1 = ((bf16[64,16,1024]{2,1,0:T(8,128)(2,1)}), bf16[64,16,1024]{2,1,0:T(8,128)(2,1)}, u32[]{:S(2)}, u32[]{:S(2)}) async-start(bf16[64,16,1024]{2,1,0:T(8,128)(2,1)} %bitcast.10), calls=%async_computation.1 | async-start | bytes 4194304 | tf_op jit(solution)/shard_map/all_to_all | solution.py:689
  136.2 1.3 copy-start.2
  137.5 14.3 %collective-permute-start.6 = (bf16[512,2048]{1,0:T(8,128)(2,1)}, bf16[512,2048]{1,0:T(8,128)(2,1)}, u32[]{:S(2)}, u32[]{:S(2)}) collective-permute-start(bf16[512,2048]{1,0:T(8,128)(2,1)} %get-tuple-element.57), channel_id=1, source_target_pairs={{0,1},{1,0},{2,3},{3,2},{4,5},{5,4},{6,7},{7,6},{8,9},{9,8},{10,11... | collective-permute-start | bytes 6291464 | tf_op jit(solution)/shard_map/ppermute | solution.py:694
  137.5 2.2 %copy-start.1 = (bf16[1024,2048]{1,0:T(8,128)(2,1)S(1)}, bf16[1024,2048]{1,0:T(8,128)(2,1)}, u32[]{:S(2)}) copy-start(bf16[1024,2048]{1,0:T(8,128)(2,1)} %get-tuple-element.50.refs_4_) | copy-start | bytes 12582916
  150.1 1.7 collective-permute-start.5
  150.7 1.2 collective-permute-start.3
  151.8 1.6 copy-start.3
  155.7 1.4 copy-start
  157.1 42.8 %all-to-all-start.2 = ((bf16[64,8,2304]{2,1,0:T(8,128)(2,1)}), bf16[64,8,2304]{2,1,0:T(8,128)(2,1)S(1)}, u32[]{:S(2)}, u32[]{:S(2)}) async-start(bf16[64,8,2304]{2,1,0:T(8,128)(2,1)} %bitcast.17), calls=%async_computation.2 | async-start | bytes 4718592 | tf_op jit(solution)/shard_map/all_to_all | solution.py:707
Sparse Core Ops, SparseCore 0:
  20.4 56.7 all-gather.1
